TPU v7x, 512 devices: a whole 4x8x8 slice. The times are simulated.
512 devices in a mesh: dp: 32 (over x, z), ctx: 16 (over y, core).
Axes of the slice: x: 4, y: 8, z: 8, core: 2. Of those that a mesh axis runs over, the one named last changes fastest.
Arguments:
- query: bfloat16 [65536, 2048], P(('dp', 'ctx')), parts along dimension 0, may hold values from -24 to 24
- key: bfloat16 [65536, 512], P(('dp', 'ctx')), parts along dimension 0, may hold values from -7.5 to 7.5
- value: bfloat16 [65536, 512], P(('dp', 'ctx')), parts along dimension 0, may hold values from -6 to 6
- output_gradient: bfloat16 [65536, 2048], P(('dp', 'ctx')), parts along dimension 0, may hold values from -6 to 6
- doc_blocks: int32 [512], P('dp'), parts along dimension 0, may hold values from 0 to 2, never falling along the last dimension, each value on 1 to 11 neighbouring positions
- shard_order: int32 [512], P('dp'), parts along dimension 0, may hold values from 0 to 15, as said below
Outputs:
- attn_out: bfloat16 [65536, 2048], P(('dp', 'ctx')), parts along dimension 0
- grad_query: bfloat16 [65536, 2048], P(('dp', 'ctx')), parts along dimension 0
- key_gradient: bfloat16 [65536, 512], P(('dp', 'ctx')), parts along dimension 0
- value_gradient: bfloat16 [65536, 512], P(('dp', 'ctx')), parts along dimension 0
There are 32 independent parts, one for each index of `dp`. A program takes and returns all parts, laid end to end along the dimension named above; each array names one. Nothing has to cross between parts.
Inputs may be any that keep to these rules, and one draw needn't show every extreme that they name: `doc_blocks`: document numbers never fall along the blocks; every document covers 1 to 11 blocks and one covers exactly 11. `shard_order`: each shard number appears once; row shard i holds shard i or shard i + 1 - 2 * (i % 2), the other member of its pair.
All inputs are finite; a program needn't handle non-finite values.
Results may differ from a plain program's by a relative error of at most 0.035.
Values may be sent and summed in bfloat16 or wider, within the bound.
No kernel may reach another device: no remote copies, remote signals or barrier semaphores. Data moves between devices by JAX's collectives and lax.ppermute only.
A program may use at most 128 MiB of HBM per device.

v0:
```python
import jax
import jax.numpy as jnp
from jax import lax
from jax.sharding import PartitionSpec as P

QUERY_HEADS = 16
KEY_VALUE_HEADS = 4
HEAD_WIDTH = 128
BLOCK = 128
QUERY_PER_KV = 4


def shards(query, key, value, output_gradient, doc_blocks, shard_order):
    token_index = query.shape[0]
    device_parts = shard_order.shape[0]
    sequence_index = token_index * device_parts
    me = lax.axis_index("ctx")
    offsets = jnp.arange(token_index, dtype=jnp.int32)
    block_ids = jnp.arange(doc_blocks.shape[0], dtype=jnp.int32)

    def doc_of(positions):
        hits = (positions // BLOCK)[..., None] == block_ids
        return jnp.sum(jnp.where(hits, doc_blocks, 0), axis=-1)

    own_shard = lax.dynamic_index_in_dim(shard_order, me, 0, keepdims=False)
    pos_own = own_shard * token_index + offsets
    doc_own = doc_of(pos_own)
    stacked_rows = jnp.stack((key, value))
    collected_rows = lax.all_gather(stacked_rows, "ctx", axis=1, tiled=True)
    block_tiles = collected_rows.reshape(2, device_parts, token_index, KEY_VALUE_HEADS, HEAD_WIDTH)
    key_pos = shard_order[:, None] * token_index + offsets[None, :]
    key_ok = jnp.ones((device_parts,), jnp.bool_)
    key_doc = doc_of(key_pos)
    allowed = (
        key_ok[:, None, None]
        & (key_doc[:, None, :] == doc_own[None, :, None])
        & (key_pos[:, None, :] <= pos_own[None, :, None])
    )
    live = jnp.any(allowed, axis=(1, 2))
    key_split = block_tiles[0]
    value_split = block_tiles[1]
    query_rows = query.reshape(token_index, KEY_VALUE_HEADS, QUERY_PER_KV, HEAD_WIDTH)
    gradient_list = output_gradient.reshape(token_index, KEY_VALUE_HEADS, QUERY_PER_KV, HEAD_WIDTH)
    scale = HEAD_WIDTH ** (-0.5)

    def scores_for(keys_blk, mask_blk):
        raw = (
            jnp.einsum("qgjd,kgd->gjqk", query_rows, keys_blk, preferred_element_type=jnp.float32)
            * scale
        )
        return jnp.where(mask_blk[None, None], raw, -jnp.inf)

    def score_block(packed):
        keys_blk, mask_blk, flag = packed
        return scores_for(keys_blk, mask_blk)

    scores = lax.map(score_block, (key_split, allowed, live))
    top = jnp.max(scores, axis=(0, 4))
    total = jnp.sum(jnp.exp(scores - top[None, ..., None]), axis=(0, 4))
    lse = top + jnp.log(total)
    attention_weights = jnp.exp(scores - lse[None, ..., None]).astype(jnp.bfloat16)
    attended = jnp.einsum(
        "ngjqk,nkgd->qgjd", attention_weights, value_split, preferred_element_type=jnp.float32
    )
    attn = attended.astype(jnp.bfloat16)
    delta = jnp.transpose(
        jnp.sum(gradient_list.astype(jnp.float32) * attn.astype(jnp.float32), axis=-1), (1, 2, 0)
    )
    second_pass = lax.all_gather(stacked_rows, "ctx", axis=1, tiled=True).reshape(
        2, device_parts, token_index, KEY_VALUE_HEADS, HEAD_WIDTH
    )
    key_back = second_pass[0]
    value_back = second_pass[1]

    def back_work(keys_blk, vals_blk, w_blk):
        dprob = jnp.einsum(
            "qgjd,kgd->gjqk", gradient_list, vals_blk, preferred_element_type=jnp.float32
        )
        score_gradient = (w_blk.astype(jnp.float32) * (dprob - delta[..., None])).astype(
            jnp.bfloat16
        )
        dq_term = jnp.einsum(
            "gjqk,kgd->qgjd", score_gradient, keys_blk, preferred_element_type=jnp.float32
        )
        dk_term = (
            jnp.einsum(
                "gjqk,qgjd->kgd", score_gradient, query_rows, preferred_element_type=jnp.float32
            )
            * scale
        )
        dv_term = jnp.einsum(
            "gjqk,qgjd->kgd", w_blk, gradient_list, preferred_element_type=jnp.float32
        )
        return (dq_term, jnp.concatenate((dk_term, dv_term), axis=1))

    def back_block(carry, packed):
        keys_blk, vals_blk, w_blk, flag = packed
        dq_term, term = back_work(keys_blk, vals_blk, w_blk)
        return (carry + dq_term, term)

    start_offset = jnp.zeros((token_index, KEY_VALUE_HEADS, QUERY_PER_KV, HEAD_WIDTH), jnp.float32)
    dq_total, term_list = lax.scan(
        back_block, start_offset, (key_back, value_back, attention_weights, live)
    )
    summed_rows = lax.psum_scatter(
        term_list.reshape(sequence_index, 2 * KEY_VALUE_HEADS * HEAD_WIDTH).astype(jnp.bfloat16),
        "ctx",
        scatter_dimension=0,
        tiled=True,
    ).astype(jnp.float32)
    key_gradient = summed_rows[:, : KEY_VALUE_HEADS * HEAD_WIDTH].astype(jnp.bfloat16)
    value_gradient = summed_rows[:, KEY_VALUE_HEADS * HEAD_WIDTH :].astype(jnp.bfloat16)
    grad_query = (
        (dq_total * scale).astype(jnp.bfloat16).reshape(token_index, QUERY_HEADS * HEAD_WIDTH)
    )
    return (
        attn.reshape(token_index, QUERY_HEADS * HEAD_WIDTH),
        grad_query,
        key_gradient,
        value_gradient,
    )


def solution(mesh):
    return jax.shard_map(
        shards,
        mesh=mesh,
        in_specs=(
            P(("dp", "ctx"), None),
            P(("dp", "ctx"), None),
            P(("dp", "ctx"), None),
            P(("dp", "ctx"), None),
            P("dp"),
            P("dp"),
        ),
        out_specs=(
            P(("dp", "ctx"), None),
            P(("dp", "ctx"), None),
            P(("dp", "ctx"), None),
            P(("dp", "ctx"), None),
        ),
        check_vma=False,
    )
```

profile of v0, /device:TPU:27, one launch (start us, length us, event | category | flops | bytes accessed | tf_op | source)
XLA Modules:
  0.0 307.6 jit_solution(855991377401946812)
XLA Ops:
  7.2 1.7 pad_maximum_fusion
  17.1 42.5 %all-gather.2.cloned.1.call-done = bf16[2,2048,512]{2,1,0:T(8,128)(2,1)} async-done(((bf16[2,128,512]{2,1,0:T(8,128)(2,1)}), bf16[2,2048,512]{2,1,0:T(8,128)(2,1)}) %all-gather.2.cloned.1.call-update) | async-done | bytes 4194320 | tf_op jit(solution)/shard_map/all_gather | solution.py:29
  59.6 4.5 %fusion.31 = (bf16[1,2048,512]{2,1,0:T(8,128)(2,1)}, bf16[1,2048,512]{2,1,0:T(8,128)(2,1)}) fusion(bf16[2,2048,512]{2,1,0:T(8,128)(2,1)} %all-gather.2.cloned.1.call-done), kind=kLoop, calls=%fused_computation.59 | loop fusion | bytes 8388608 | tf_op jit(solution)/shard_map/slice | solution.py:41
  64.1 4.0 %reshape.129 = bf16[16,128,4,128]{3,2,1,0:T(4,128)(2,1)} reshape(bf16[1,2048,512]{2,1,0:T(8,128)(2,1)} %get-tuple-element.197) | data formatting | bytes 4194304 | tf_op jit(solution)/shard_map/squeeze | solution.py:40
  68.1 36.5 %while.23 = (s32[]{:T(128)}, f32[16,4,4,128,128]{3,4,2,1,0:T(8,128)}, pred[16,128,128]{1,2,0:T(8,128)(4,1)S(1)}, bf16[16,128,4,128]{3,2,1,0:T(4,128)(2,1)}, bf16[128,4,4,128]{3,0,2,1:T(8,128)(2,1)S(1)}, /*index=5*/s32[]{:T(128)}) while((s32[]{:T(128)}, f32[16,4,4,128,128]{3,4,2,1,0:T(8,128)}, pred[16,128,128]{1,2,0:T(8,128)(4,1)S(1)}, ...), condition=%wide.region_3.4_spmd, body=%wide.region_2.3_spmd.sunk | while | flops 67633152 | bytes 2015821 | solution.py:57
  71.3 1.3 fusion.53
  87.3 1.4 fusion.53
  96.4 1.4 fusion.53
  104.6 7.3 %reduce_max.9 = f32[4,4,128]{2,1,0:T(4,128)S(1)} reduce(f32[16,4,4,128,128]{3,4,2,1,0:T(8,128)} %get-tuple-element.79, f32[]{:T(128)} %constant.74.clone.1), dimensions={0,4}, to_apply=%region_4.5 | reduce | flops 4192256 | bytes 16785412 | tf_op jit(solution)/shard_map/reduce_max | solution.py:58
  111.9 8.0 %exponential_reduce_fusion = f32[4,4,128]{2,1,0:T(4,128)S(1)} fusion(f32[16,4,4,128,128]{3,4,2,1,0:T(8,128)} %get-tuple-element.79, f32[4,4,128]{2,1,0:T(4,128)S(1)} %reduce_max.9), kind=kLoop, calls=%fused_computation.28 | loop fusion | flops 8386560 | bytes 16793600 | tf_op jit(solution)/shard_map/reduce_sum | solution.py:59
  119.8 9.7 %exponential_convert_fusion = bf16[16,4,4,128,128]{3,4,2,1,0:T(8,128)(2,1)} fusion(f32[16,4,4,128,128]{3,4,2,1,0:T(8,128)} %get-tuple-element.79, f32[4,4,128]{2,1,0:T(4,128)S(1)} %bitcast.150), kind=kLoop, calls=%fused_computation.27 | loop fusion | flops 8388608 | bytes 25174016 | tf_op jit(solution)/shard_map/convert_element_type | solution.py:61
  129.5 4.0 %reshape.128 = bf16[16,128,4,128]{3,2,1,0:T(4,128)(2,1)} reshape(bf16[1,2048,512]{2,1,0:T(8,128)(2,1)} %get-tuple-element.196) | data formatting | bytes 4194304 | tf_op jit(solution)/shard_map/squeeze | solution.py:41
  133.5 5.4 %multiply_reduce_fusion = (f32[128,4,4]{0,2,1:T(4,128)S(1)}, bf16[4,128,4,128]{3,1,2,0:T(8,128)(2,1)S(1)}) fusion(bf16[128,2048]{0,1:T(8,128)(2,1)S(1)} %copy.43, bf16[16,4,4,128,128]{3,4,2,1,0:T(8,128)(2,1)} %exponential_convert_fusion, bf16[16,128,4,128,1]{3,2,1,0,4:T(4,128)(2,1)} %bitcast.140), kind=kOutput, calls=%fused_computation.36 | convolution fusion | flops 1075050496 | bytes 11542528 | tf_op jit(solution)/shard_map/ngjqk,nkgd->qgjd/dot_general | solution.py:62
  138.9 86.5 %while.24 = (s32[]{:T(128)}, f32[128,4,4,128]{0,3,2,1:T(8,128)S(1)}, bf16[16,128,8,128]{3,1,2,0:T(8,128)(2,1)}, bf16[16,128,4,128]{3,2,1,0:T(4,128)(2,1)}, bf16[...) while((s32[]{:T(128)}, ...), condition=%wide.region_8.9_spmd.clone, body=%wide.region_7.8_spmd.clone.sunk | while | flops 270663680 | bytes 8135807 | solution.py:102
  140.0 1.3 fusion.61
  141.7 1.3 convolution_bitcast_fusion.5
  145.4 1.3 fusion.61
  147.0 1.3 convolution_bitcast_fusion.5
  150.8 1.3 fusion.61
  152.4 1.3 convolution_bitcast_fusion.5
  156.2 1.3 fusion.61
  157.8 1.3 convolution_bitcast_fusion.5
  161.6 1.3 fusion.61
  163.2 1.3 convolution_bitcast_fusion.5
  167.0 1.3 fusion.61
  168.6 1.3 convolution_bitcast_fusion.5
  172.4 1.3 fusion.61
  174.0 1.3 convolution_bitcast_fusion.5
  177.8 1.3 fusion.61
  179.4 1.3 convolution_bitcast_fusion.5
  183.2 1.3 fusion.61
  184.8 1.3 convolution_bitcast_fusion.5
  188.6 1.3 fusion.61
  190.2 1.3 convolution_bitcast_fusion.5
  194.0 1.3 fusion.61
  195.6 1.3 convolution_bitcast_fusion.5
  199.4 1.3 fusion.61
  204.8 1.3 fusion.61
  206.4 1.3 convolution_bitcast_fusion.5
  210.1 1.3 fusion.61
  211.8 1.3 convolution_bitcast_fusion.5
  215.5 1.3 fusion.61
  220.9 1.3 fusion.61
  222.6 1.3 convolution_bitcast_fusion.5
  225.4 5.7 %copy.49 = bf16[16,128,8,128]{3,2,1,0:T(8,128)(2,1)S(1)} copy(bf16[16,128,8,128]{3,1,2,0:T(8,128)(2,1)} %get-tuple-element.81) | data formatting | bytes 8388608 | tf_op jit(solution)/shard_map/convert_element_type | solution.py:106
  231.2 3.0 copy.95
  236.4 62.8 %reduce-scatter.2.cloned.1.call-done = bf16[128,1024]{1,0:T(8,128)(2,1)} async-done(((bf16[2048,1024]{1,0:T(8,128)(2,1)}), bf16[128,1024]{1,0:T(8,128)(2,1)}) %reduce-scatter.2.cloned.1.call-update) | async-done | bytes 262160 | tf_op jit(solution)/shard_map/reduce_scatter | solution.py:105
  299.1 1.7 fusion.32
  (150 shorter events, 87.2 us)
Async XLA Ops:
  7.2 52.4 %all-gather.2.cloned.1.call-start = ((), (), s32[]{:S(2)}) async-start(), calls=%async_computation.1 | async-start | bytes 4456448 | tf_op jit(solution)/shard_map/all_gather | solution.py:29
  8.9 290.2 %reduce-scatter.2.cloned.1.call-start = ((), (), s32[]{:S(2)}) async-start(), calls=%async_computation.2 | async-start | bytes 4456448 | tf_op jit(solution)/shard_map/reduce_scatter | solution.py:105
Sparse Core Ops, SparseCore 0:
  10.7 48.8 all-gather.1
  234.3 64.7 reduce-scatter.1
where the time goes:
time: 310 us; the launch traced here: 308 us
  waiting for transfers between devices  105 us (34%)
  matrix products  80.9 us (26%)
  local copies, waits for them, and re-layouts  63.9 us (21%)
  other arithmetic  41.5 us (13%)
  between operations  14.8 us (5%)
    reduce_scatter x1, waiting for transfers between devices, shards(): lax.psum_scatter(term_list.reshape(sequence_index, 2 * KEY_VALUE_HEADS *...  62.8 us
    all_gather x1, waiting for transfers between devices, shards(): collected_rows = lax.all_gather(stacked_rows, 'ctx', axis=1, tiled=True)  42.5 us
    dynamic_slice x48, local copies, waits for them, and re-layouts, shards(): scores = lax.map(score_block, (key_split, allowed, live))  34.4 us
    dot_general x16, matrix products, back_work(): jnp.einsum('qgjd,kgd->gjqk', gradient_list, vals_blk, preferred_element_t...  21.5 us
    dot_general x16, matrix products, back_work(): jnp.einsum('gjqk,qgjd->kgd', w_blk, gradient_list, preferred_element_type...  21.3 us
    dot_general x16, matrix products, scores_for(): jnp.einsum('qgjd,kgd->gjqk', query_rows, keys_blk, preferred_element_type...  20.9 us
    dynamic_update_slice x16, other arithmetic, shards(): lax.scan(back_block, start_offset, (key_back, value_back, attention_weigh...  11.8 us
    convert_element_type x1, other arithmetic, shards(): jnp.exp(scores - lse[None, ..., None]).astype(jnp.bfloat16)  9.67 us
  transfers between devices with their start and end apart: 2, of which 2 were waited for; matrix products, arithmetic and copies ran while one was open for 3% of the time, Pallas kernels for 0%

commit v1 on v0

v1 whole, which is shorter than its diff:
```python
import jax
import jax.numpy as jnp
from jax import lax
from jax.experimental import pallas as pl
from jax.experimental.pallas import tpu as pltpu
from jax.sharding import PartitionSpec as P

GROUPS = 4
PER = 4
D = 128
T = 128
UNIT = 256
MAXU = 6
BLOCKS = 16
SCALE = D ** -0.5
LOG2E = 1.4426950408889634
FAR = 1 << 24


def nt(a, b):
    return lax.dot_general(a, b, (((1,), (1,)), ((), ())), preferred_element_type=jnp.float32)


def tn(a, b):
    return lax.dot_general(a, b, (((0,), (0,)), ((), ())), preferred_element_type=jnp.float32)


def nn(a, b):
    return lax.dot_general(a, b, (((1,), (0,)), ((), ())), preferred_element_type=jnp.float32)


def kernel(docs, order, place, q_ref, do_ref, k_ref, v_ref, o_ref, dq_ref, dkv_ref, e_buf):
    rows = PER * T
    own = order[place[0]]
    own_doc = docs[own]
    first = sum((docs[b] < own_doc).astype(jnp.int32) for b in range(BLOCKS)) >> 1
    count = (own >> 1) - first + 1
    base = own * T

    def start_of(row):
        s = order[row]
        return jnp.where(docs[s] == own_doc, s * T, FAR)

    q = jnp.concatenate([q_ref[:, j * D:(j + 1) * D] for j in range(PER)], axis=0)
    do = jnp.concatenate([do_ref[:, j * D:(j + 1) * D] for j in range(PER)], axis=0)
    do_t = do.astype(jnp.float32).T
    q_pos = base + lax.rem(lax.broadcasted_iota(jnp.int32, (1, rows), 1), T)
    half = lax.broadcasted_iota(jnp.int32, (UNIT, 1), 0)

    def fold_max(a):
        return jnp.max(a.reshape(UNIT // 8, 8, rows), axis=0)

    def fold_sum(a):
        return jnp.sum(a.reshape(UNIT // 8, 8, rows), axis=0)

    def score(i, top):
        u = first + i
        at = pl.multiple_of(u * UNIT, UNIT)
        s = nt(k_ref[pl.ds(at, UNIT), :], q)
        k_pos = jnp.where(half < T, start_of(2 * u) + half, start_of(2 * u + 1) + half - T)
        s = jnp.where(k_pos <= q_pos, s, -jnp.inf)
        e_buf[pl.ds(pl.multiple_of(i * UNIT, UNIT), UNIT), :] = s
        return jnp.maximum(top, fold_max(s))

    top8 = lax.fori_loop(0, count, score, jnp.full((8, rows), -jnp.inf, jnp.float32))
    top = jnp.max(top8, axis=0, keepdims=True)

    def weigh(i, carry):
        total, out_t = carry
        at = pl.multiple_of((first + i) * UNIT, UNIT)
        sl = pl.ds(pl.multiple_of(i * UNIT, UNIT), UNIT)
        e = jnp.exp2((e_buf[sl, :] - top) * (SCALE * LOG2E))
        e_buf[sl, :] = e
        v = v_ref[pl.ds(at, UNIT), :]
        return total + fold_sum(e), out_t + tn(v, e.astype(jnp.bfloat16))

    total8, out_t = lax.fori_loop(
        0, count, weigh, (jnp.zeros((8, rows), jnp.float32), jnp.zeros((D, rows), jnp.float32))
    )
    inv = 1.0 / jnp.sum(total8, axis=0, keepdims=True)
    attn_t = (out_t * inv).astype(jnp.bfloat16).astype(jnp.float32)
    delta = jnp.sum(attn_t * do_t, axis=0, keepdims=True)
    for j in range(PER):
        o_ref[:, j * D:(j + 1) * D] = attn_t[:, j * T:(j + 1) * T].T.astype(jnp.bfloat16)

    dkv_ref[...] = jnp.zeros_like(dkv_ref)

    def back(i, dq_t):
        at = pl.multiple_of((first + i) * UNIT, UNIT)
        sl = pl.ds(pl.multiple_of(i * UNIT, UNIT), UNIT)
        k = k_ref[pl.ds(at, UNIT), :]
        v = v_ref[pl.ds(at, UNIT), :]
        w = e_buf[sl, :] * inv
        dp = nt(v, do)
        ds = (w * (dp - delta)).astype(jnp.bfloat16)
        dkv_ref[pl.ds(at, UNIT), :D] = (nn(ds, q) * SCALE).astype(jnp.bfloat16)
        dkv_ref[pl.ds(at, UNIT), D:] = nn(w.astype(jnp.bfloat16), do).astype(jnp.bfloat16)
        return dq_t + tn(k, ds)

    dq_t = lax.fori_loop(0, count, back, jnp.zeros((D, rows), jnp.float32)) * SCALE
    for j in range(PER):
        dq_ref[:, j * D:(j + 1) * D] = dq_t[:, j * T:(j + 1) * T].T.astype(jnp.bfloat16)


def shards(query, key, value, output_gradient, doc_blocks, shard_order):
    me = lax.axis_index("ctx")
    kv = jnp.concatenate((key, value), axis=1)
    kv_all = lax.all_gather(kv, "ctx", axis=0, tiled=True)
    tokens = kv_all.shape[0]
    attn, grad_query, dkv = pl.pallas_call(
        kernel,
        grid_spec=pltpu.PrefetchScalarGridSpec(
            num_scalar_prefetch=3,
            grid=(GROUPS,),
            in_specs=[
                pl.BlockSpec((T, PER * D), lambda g, *_: (0, g)),
                pl.BlockSpec((T, PER * D), lambda g, *_: (0, g)),
                pl.BlockSpec((tokens, D), lambda g, *_: (0, g)),
                pl.BlockSpec((tokens, D), lambda g, *_: (0, GROUPS + g)),
            ],
            out_specs=[
                pl.BlockSpec((T, PER * D), lambda g, *_: (0, g)),
                pl.BlockSpec((T, PER * D), lambda g, *_: (0, g)),
                pl.BlockSpec((tokens, 2 * D), lambda g, *_: (0, g)),
            ],
            scratch_shapes=[pltpu.VMEM((MAXU * UNIT, PER * T), jnp.float32)],
        ),
        out_shape=[
            jax.ShapeDtypeStruct(query.shape, jnp.bfloat16),
            jax.ShapeDtypeStruct(query.shape, jnp.bfloat16),
            jax.ShapeDtypeStruct((tokens, 2 * GROUPS * D), jnp.bfloat16),
        ],
        compiler_params=pltpu.CompilerParams(
            dimension_semantics=("arbitrary",), vmem_limit_bytes=56 * 1024 * 1024
        ),
        name="attention",
    )(doc_blocks, shard_order, me.reshape(1), query, output_gradient, kv_all, kv_all)
    grads = lax.psum_scatter(dkv, "ctx", scatter_dimension=0, tiled=True)
    return (
        attn,
        grad_query,
        jnp.concatenate([grads[:, 2 * D * g:2 * D * g + D] for g in range(GROUPS)], axis=1),
        jnp.concatenate([grads[:, 2 * D * g + D:2 * D * g + 2 * D] for g in range(GROUPS)], axis=1),
    )


def solution(mesh):
    rows = P(("dp", "ctx"), None)
    return jax.shard_map(
        shards,
        mesh=mesh,
        in_specs=(rows, rows, rows, rows, P("dp"), P("dp")),
        out_specs=(rows, rows, rows, rows),
        check_vma=False,
    )
```

time: 310 us -> 161 us (0.52)
  matrix products: 80.9 us -> 0 us
  local copies, waits for them, and re-layouts: 63.9 us -> 0.89 us
  other arithmetic: 41.5 us -> 2.43 us
  waiting for transfers between devices: 105 us -> 130 us
  Pallas kernels: 0 us -> 12.9 us
    dot_general x81 -> x0, matrix products: 80.9 us -> none  [the longest x16 21.5 us: back_work(): jnp.einsum('qgjd,kgd->gjqk', gradient_list, vals_blk, preferred_element_t...]
    dynamic_slice x49 -> x0, local copies, waits for them, and re-layouts: 35.7 us -> none  [the longest x48 34.4 us: shards(): scores = lax.map(score_block, (key_split, allowed, live))]
    reduce_scatter x1, waiting for transfers between devices: 62.8 us -> 79.4 us  [shards(): grads = lax.psum_scatter(dkv, 'ctx', scatter_dimension=0, tiled=True)]
    pallas_call x0 -> x1, Pallas kernels: none -> 12.9 us  [shards(): pl.pallas_call(kernel, grid_spec=pltpu.PrefetchScalarGridSpec(num_scalar_...]
    dynamic_update_slice x16 -> x0, other arithmetic: 11.8 us -> none  [shards(): lax.scan(back_block, start_offset, (key_back, value_back, attention_weigh...]
    convert_element_type x2 -> x0, other arithmetic: 9.8 us -> none  [the longest x1 9.67 us: shards(): jnp.exp(scores - lse[None, ..., None]).astype(jnp.bfloat16)]
    reduce_sum x3 -> x0, other arithmetic: 9.48 us -> none  [the longest x1 7.98 us: shards(): total = jnp.sum(jnp.exp(scores - top[None, ..., None]), axis=(0, 4))]
    all_gather x1, waiting for transfers between devices: 42.5 us -> 50.5 us  [shards(): kv_all = lax.all_gather(kv, 'ctx', axis=0, tiled=True)]
  transfers between devices with their start and end apart: 2 -> 2, of which waited for: 2 -> 2; matrix products, arithmetic and copies ran while one was open for 3% -> 0% of each run, Pallas kernels for 0% -> 0%
where the time goes in v1:
time: 161 us; the launch traced here: 160 us
  waiting for transfers between devices  130 us (81%)
  between operations  14 us (9%)
  Pallas kernels  12.9 us (8%)
  other arithmetic  2.43 us (2%)
    reduce_scatter x1, waiting for transfers between devices, shards(): grads = lax.psum_scatter(dkv, 'ctx', scatter_dimension=0, tiled=True)  79.4 us
    all_gather x1, waiting for transfers between devices, shards(): kv_all = lax.all_gather(kv, 'ctx', axis=0, tiled=True)  50.5 us
    pallas_call x1, Pallas kernels, shards(): pl.pallas_call(kernel, grid_spec=pltpu.PrefetchScalarGridSpec(num_scalar_...  12.9 us
  transfers between devices with their start and end apart: 2, of which 2 were waited for; matrix products, arithmetic and copies ran while one was open for 0% of the time, Pallas kernels for 0%

profile of v1, /device:TPU:27, one launch (start us, length us, event | category | flops | bytes accessed | tf_op | source)
XLA Modules:
  0.0 160.3 jit_solution(7287733713088857274)
XLA Ops:
  7.2 0.0 all-gather.2.cloned.1.call-start
  7.2 1.7 %pad_maximum_fusion = bf16[128,1024]{1,0:T(8,128)(2,1)} fusion(bf16[128,512]{1,0:T(8,128)(2,1)} %param.8, bf16[128,512]{1,0:T(8,128)(2,1)} %param.7), kind=kLoop, calls=%fused_computation | loop fusion | flops 524288 | bytes 524288 | tf_op jit(solution)/shard_map/concatenate | solution.py:107
  8.9 0.0 all-gather.2.cloned.1.call-update
  8.9 0.0 reduce-scatter.2.cloned.1.call-start
  9.0 50.5 %all-gather.2.cloned.1.call-done.k_ref.v_ref = bf16[2048,1024]{1,0:T(8,128)(2,1)} async-done(((bf16[128,1024]{1,0:T(8,128)(2,1)}), bf16[2048,1024]{1,0:T(8,128)(2,1)}) %all-gather.2.cloned.1.call-update) | async-done | bytes 4194320 | tf_op jit(solution)/shard_map/all_gather | solution.py:108
  59.5 12.9 %attention.1 = (bf16[128,2048]{1,0:T(8,128)(2,1)}, bf16[128,2048]{1,0:T(8,128)(2,1)}, bf16[2048,1024]{1,0:T(8,128)(2,1)}) custom-call(s32[16]{0:T(128)} %docs.1, s32[16]{0:T(128)} %order.1, s32[1]{0:T(128)} %bitcast.place, bf16[128,2048]{1,0:T(8,128)(2,1)} %q_ref.1, bf16[128,2048]{1,0:T(8,128)(2,1)} %do_ref.1, ...), custom_call_target="tpu_custom_call" | custom-call | tf_op jit(solution)/shard_map/attention/pallas_call | solution.py:110
  72.4 0.0 reduce-scatter.2.cloned.1.call-update
  72.4 79.4 %reduce-scatter.2.cloned.1.call-done = bf16[128,1024]{1,0:T(8,128)(2,1)} async-done(((bf16[2048,1024]{1,0:T(8,128)(2,1)}), bf16[128,1024]{1,0:T(8,128)(2,1)}) %reduce-scatter.2.cloned.1.call-update) | async-done | bytes 262160 | tf_op jit(solution)/shard_map/reduce_scatter | solution.py:138
  151.9 0.9 fusion
  152.8 0.7 pad_maximum_fusion.1
Async XLA Ops:
  7.2 52.4 %all-gather.2.cloned.1.call-start = ((), (), s32[]{:S(2)}) async-start(), calls=%async_computation.1 | async-start | bytes 4456448 | tf_op jit(solution)/shard_map/all_gather | solution.py:108
  8.9 142.9 %reduce-scatter.2.cloned.1.call-start = ((), (), s32[]{:S(2)}) async-start(), calls=%async_computation.2 | async-start | bytes 4456448 | tf_op jit(solution)/shard_map/reduce_scatter | solution.py:138
Sparse Core Ops, SparseCore 0:
  10.7 48.7 all-gather.1
  72.5 79.2 reduce-scatter.1

commit v2 on v1

v2 whole, which is shorter than its diff:
```python
import functools

import jax
import jax.numpy as jnp
from jax import lax
from jax.experimental import pallas as pl
from jax.experimental.pallas import tpu as pltpu
from jax.sharding import PartitionSpec as P

D = 128
T = 128
UNIT = 256
ROWS = 512
CHUNKS = 4
HALF_Q = 1024
HALF_KV = 256
CHIPS = 8
SCALE = D ** -0.5
FACTOR = SCALE * 1.4426950408889634
INF = float("inf")


def nt(a, b):
    return lax.dot_general(a, b, (((1,), (1,)), ((), ())), preferred_element_type=jnp.float32)


def tn(a, b):
    return lax.dot_general(a, b, (((0,), (0,)), ((), ())), preferred_element_type=jnp.float32)


def nn(a, b):
    return lax.dot_general(a, b, (((1,), (0,)), ((), ())), preferred_element_type=jnp.float32)


def fold_max(a):
    return jnp.max(a.reshape(a.shape[0] // 8, 8, a.shape[1]), axis=0)


def fold_sum(a):
    return jnp.sum(a.reshape(a.shape[0] // 8, 8, a.shape[1]), axis=0)


def dead_terms(docs, order, me, distance):
    there = jnp.maximum(me - 2 * distance, me & 1)
    keys = (order[there], order[there ^ 1])
    queries = (order[me], order[me ^ 1])
    near = me >= 2 * distance

    def meets(k, q):
        return near & (docs[k] == docs[q]) & (k <= q)

    table = [[meets(k, q) for k in keys] for q in queries]
    alive = table[0][0] | table[0][1] | table[1][0] | table[1][1]
    return [[jnp.where(m, 0.0, INF) for m in row] for row in table], alive


def columns(h, base=0):
    return pl.ds(pl.multiple_of(base + h * D, D), D)


def causal():
    k = lax.broadcasted_iota(jnp.int32, (T, ROWS), 0)
    q = lax.rem(lax.broadcasted_iota(jnp.int32, (T, ROWS), 1), T)
    return k <= q


def both(a, b):
    return jnp.concatenate([a, b], axis=0)


def forward_unit(u_ref, q_ref, m_ref, l_ref, acc_ref, dead):
    def head(h, _):
        k, v = u_ref[:, columns(h)], u_ref[:, columns(h, HALF_KV)]
        for half in range(2):
            chunk = 2 * h + half
            s = nt(k, q_ref[chunk])
            d0, d1 = dead[half]
            peak = jnp.maximum(fold_max(s[:T]) - d0, fold_max(s[T:]) - d1)
            old = m_ref[chunk]
            new = jnp.maximum(old, jnp.max(peak, axis=0, keepdims=True))
            m_ref[chunk] = new
            fade = jnp.exp2((old - new) * FACTOR)
            shift = new[:1] * FACTOR
            e0 = jnp.exp2(s[:T] * FACTOR - (shift + d0))
            e1 = jnp.exp2(s[T:] * FACTOR - (shift + d1))
            l_ref[chunk] = l_ref[chunk] * fade + fold_sum(e0) + fold_sum(e1)
            acc_ref[chunk] = acc_ref[chunk] * fade[:1] + tn(v, both(e0, e1).astype(jnp.bfloat16))
        return 0

    lax.fori_loop(0, 2, head, 0, unroll=True)


def backward_unit(u_ref, q_ref, do_ref, lse_ref, delta_ref, dq_ref, g_ref, dead, own):
    def head(h, _):
        k, v = u_ref[:, columns(h)], u_ref[:, columns(h, HALF_KV)]
        dk = dv = None
        for half in range(2):
            chunk = 2 * h + half
            q, do = q_ref[chunk], do_ref[chunk]
            s = nt(k, q)
            shift, delta = lse_ref[chunk][:1], delta_ref[chunk][:1]
            w = [jnp.exp2(s[T * i:T * i + T] * FACTOR - (shift + dead[half][i])) for i in range(2)]
            if own:
                w[half] = jnp.where(causal(), w[half], 0.0)
            w = both(*w)
            ds = (w * (nt(v, do) - delta)).astype(jnp.bfloat16)
            k_term = nn(ds, q)
            v_term = nn(w.astype(jnp.bfloat16), do)
            dk = k_term if dk is None else dk + k_term
            dv = v_term if dv is None else dv + v_term
            dq_ref[chunk] += tn(k, ds)
        g_ref[:, columns(h)] = (dk * SCALE).astype(jnp.bfloat16)
        g_ref[:, columns(h, HALF_KV)] = dv.astype(jnp.bfloat16)
        return 0

    lax.fori_loop(0, 2, head, 0, unroll=True)


def first_kernel(docs, order, place, q_own, do_own, other, u_ref, q_ref, do_ref, m_ref, l_ref, acc_ref):
    me = place[0]
    dead, _ = dead_terms(docs, order, me, 0)
    sides = ((q_own, do_own), (other.at[:, :HALF_Q], other.at[:, HALF_Q:2 * HALF_Q]))

    for h in range(2):
        k, v = u_ref[:, h * D:(h + 1) * D], u_ref[:, HALF_KV + h * D:HALF_KV + (h + 1) * D]
        for half in range(2):
            chunk = 2 * h + half
            for source, target in zip(sides[half], (q_ref, do_ref)):
                for j in range(4):
                    target[chunk, j * T:(j + 1) * T, :] = source[:, (4 * h + j) * D:(4 * h + j + 1) * D]
            s = nt(k, q_ref[chunk])
            part = [s[:T], s[T:]]
            part[half] = jnp.where(causal(), part[half], -INF)
            part[1 - half] = part[1 - half] - dead[half][1 - half]
            s = both(*part)
            top = jnp.max(fold_max(s), axis=0, keepdims=True)
            e = jnp.exp2((s - top) * FACTOR)
            m_ref[chunk] = jnp.broadcast_to(top, (8, ROWS))
            l_ref[chunk] = fold_sum(e)
            acc_ref[chunk] = tn(v, e.astype(jnp.bfloat16))


def near_kernel(units, docs, order, place, q_ref, m_in, l_in, acc_in, *refs):
    n = len(units)
    m_ref, l_ref, acc_ref = refs[n:]
    m_ref[...] = m_in[...]
    l_ref[...] = l_in[...]
    acc_ref[...] = acc_in[...]
    forward_units(units, refs[:n], docs, order, place[0], q_ref, m_ref, l_ref, acc_ref)


def forward_units(units, u_refs, docs, order, me, q_ref, m_ref, l_ref, acc_ref):
    for distance, u_ref in zip(units, u_refs):
        dead, alive = dead_terms(docs, order, me, distance)

        @pl.when(alive)
        def _():
            forward_unit(u_ref, q_ref, m_ref, l_ref, acc_ref, dead)


def middle_kernel(docs, order, place, q_ref, do_ref, m_in, l_in, acc_in, u3, u4, o_own, o_send, lse_ref, delta_ref, dq_ref, g3, g4, m_ref, l_ref, acc_ref):
    me = place[0]
    m_ref[...] = m_in[...]
    l_ref[...] = l_in[...]
    acc_ref[...] = acc_in[...]
    forward_units((3, 4), (u3, u4), docs, order, me, q_ref, m_ref, l_ref, acc_ref)
    for chunk in range(CHUNKS):
        total = jnp.sum(l_ref[chunk], axis=0, keepdims=True)
        attn = (acc_ref[chunk] * (1.0 / total)).astype(jnp.bfloat16).astype(jnp.float32)
        do_t = do_ref[chunk].astype(jnp.float32).T
        lse_ref[chunk] = m_ref[chunk] * FACTOR + jnp.log2(total)
        delta_ref[chunk] = jnp.broadcast_to(jnp.sum(attn * do_t, axis=0, keepdims=True), (8, ROWS))
        out = (o_own, o_send)[chunk % 2]
        for j in range(4):
            at = (chunk // 2 * 4 + j) * D
            out[:, at:at + D] = attn[:, j * T:(j + 1) * T].T.astype(jnp.bfloat16)
    dq_ref[...] = jnp.zeros_like(dq_ref)
    backward_units((4, 3), (u4, u3), (g4, g3), docs, order, me, q_ref, do_ref, lse_ref, delta_ref, dq_ref)


def backward_units(units, u_refs, g_refs, docs, order, me, q_ref, do_ref, lse_ref, delta_ref, dq_ref):
    for distance, u_ref, g_ref in zip(units, u_refs, g_refs):
        dead, alive = dead_terms(docs, order, me, distance)

        @pl.when(alive)
        def _():
            backward_unit(u_ref, q_ref, do_ref, lse_ref, delta_ref, dq_ref, g_ref, dead, distance == 0)

        if distance > 0:
            @pl.when(jnp.logical_not(alive))
            def _():
                g_ref[...] = jnp.zeros_like(g_ref)


def back_kernel(units, docs, order, place, *refs):
    q_ref, do_ref, lse_ref, delta_ref, dq_in = refs[:5]
    n = len(units)
    final = 0 in units
    u_refs, outs = refs[5:5 + n], refs[5 + n + final:]
    g_refs = outs[:n]
    dq_ref = outs[-1]
    me = place[0]
    dq_ref[...] = dq_in[...]
    backward_units(units, u_refs, g_refs, docs, order, me, q_ref, do_ref, lse_ref, delta_ref, dq_ref)
    if final:
        o_send, packed = refs[5 + n], outs[n + 1]
        packed[:, :HALF_Q] = o_send[...]
        for chunk in range(CHUNKS):
            dq = dq_ref[chunk] * SCALE
            for j in range(4):
                at = (chunk // 2 * 4 + j) * D
                tile = dq[:, j * T:(j + 1) * T].T.astype(jnp.bfloat16)
                if chunk % 2 == 0:
                    outs[n][:, at:at + D] = tile
                else:
                    packed[:, HALF_Q + at:HALF_Q + at + D] = tile


def call(body, name, scalars, operands, specs, outs, scratch=()):
    whole = lambda shape: pl.BlockSpec(shape, lambda i, *_: (0,) * len(shape))
    return pl.pallas_call(
        body,
        grid_spec=pltpu.PrefetchScalarGridSpec(
            num_scalar_prefetch=3,
            grid=(1,),
            in_specs=[whole(a.shape) if s is None else s for a, s in zip(operands, specs)],
            out_specs=[whole(o.shape) for o in outs],
            scratch_shapes=list(scratch),
        ),
        out_shape=list(outs),
        cost_estimate=pl.CostEstimate(flops=1024, bytes_accessed=1024, transcendentals=0),
        compiler_params=pltpu.CompilerParams(
            dimension_semantics=("arbitrary",), vmem_limit_bytes=40 * 1024 * 1024
        ),
        name=name,
    )(*scalars, *operands)


def hop(x, pairs, cross=0):
    return lax.ppermute(x, "ctx", [(2 * a + c, 2 * b + (c ^ cross)) for a, b in pairs for c in range(2)])


def after(x, *others):
    return lax.optimization_barrier((x,) + others)[0]


def swap(x):
    return lax.ppermute(x, "ctx", [(i, i ^ 1) for i in range(2 * CHIPS)])


def struct(shape, dtype=jnp.float32):
    return jax.ShapeDtypeStruct(shape, dtype)


def shards(query, key, value, output_gradient, doc_blocks, shard_order):
    me = lax.axis_index("ctx")
    core = me & 1
    scalars = (doc_blocks, shard_order, me.reshape(1))

    def side(x, which, width):
        return lax.dynamic_slice_in_dim(x, which * width, width, axis=1)

    kv_own = jnp.concatenate((side(key, core, HALF_KV), side(value, core, HALF_KV)), axis=1)
    across = swap(jnp.concatenate(
        (side(query, 1 - core, HALF_Q), side(output_gradient, 1 - core, HALF_Q), side(key, 1 - core, HALF_KV), side(value, 1 - core, HALF_KV)),
        axis=1,
    ))
    u0 = jnp.concatenate((kv_own, across[:, 2 * HALF_Q:]), axis=0)
    u6 = hop(u0, [(s, (s + 6) % CHIPS) for s in range(4)])
    u1 = hop(u0, [(s, s + 1) for s in range(7)])
    u5 = hop(u6, [((s + 6) % CHIPS, (s + 5) % CHIPS) for s in range(4)])
    u2 = hop(u1, [(s, s + 1) for s in range(1, 7)])
    u3 = hop(u2, [(s, s + 1) for s in range(2, 7)])
    u4 = hop(u5, [(s, (s - 1) % CHIPS) for s in (5, 6, 7, 0)])

    mine = pl.BlockSpec((T, HALF_Q), lambda i, d, o, p: (0, p[0] & 1))
    stats = struct((CHUNKS, 8, ROWS))
    wide = struct((CHUNKS, D, ROWS))
    stacked = struct((CHUNKS, ROWS, D), jnp.bfloat16)
    unit = struct((UNIT, 2 * HALF_KV), jnp.bfloat16)
    packed = struct((T, 2 * HALF_Q), jnp.bfloat16)
    token_half = struct((T, HALF_Q), jnp.bfloat16)
    held = [pltpu.VMEM(x.shape, x.dtype) for x in (stats, stats, wide)]

    q, do, m0, l0, acc0 = call(
        first_kernel, "own", scalars, (query, output_gradient, across, u0),
        (mine, mine, None, None), (stacked, stacked, stats, stats, wide),
    )
    m1, l1, acc1 = call(
        functools.partial(near_kernel, (1, 2)), "near", scalars, (q, m0, l0, acc0, u1, u2), (None,) * 6,
        (stats, stats, wide),
    )
    m2, l2, acc2 = call(
        functools.partial(near_kernel, (5,)), "far", scalars, (q, m1, l1, acc1, u5), (None,) * 5,
        (stats, stats, wide),
    )
    o_own, o_send, lse, delta, dq3, g3, g4 = call(
        middle_kernel, "middle", scalars, (q, do, m2, l2, acc2, u3, u4), (None,) * 7,
        (token_half, token_half, stats, stats, wide, unit, unit), held,
    )

    def back(units, name, dq, held_units):
        n = len(units)
        outs = (unit,) * n + ((token_half, packed) if 0 in units else (wide,))
        return call(
            functools.partial(back_kernel, units), name, scalars, (q, do, lse, delta, dq, *held_units),
            (None,) * (5 + len(held_units)), outs, held[2:] if 0 in units else (),
        )

    def add(*terms):
        total = terms[0].astype(jnp.float32)
        for term in terms[1:]:
            total = total + term.astype(jnp.float32)
        return total.astype(jnp.bfloat16)

    b4 = hop(g4, [(t, (t + 1) % CHIPS) for t in range(4, 8)])
    b3 = hop(g3, [(t, t - 1) for t in range(3, 8)])
    g5, g2, dq2 = back((5, 2), "back52", dq3, (u5, u2))
    a5 = add(g5, b4)
    a2 = add(g2, b3)
    r5 = hop(a5, [(t, (t + 3) % CHIPS) for t in (5, 6, 7, 0)])
    b2 = hop(a2, [(t, t - 1) for t in range(2, 8)])
    g1, g0, dq_own, sent = back((1, 0), "back10", after(dq2, a5, a2), (u1, u0, o_send))
    a1 = add(g1, b2)
    r1 = [hop(a1[i * T:(i + 1) * T], [(t, t - 1) for t in range(1, 8)], i) for i in range(2)]
    other = swap(sent)
    s05 = add(g0, r5)
    s05_other = swap(s05[T:])

    def join(own, other):
        return jnp.where(core == 0, jnp.concatenate((own, other), axis=1), jnp.concatenate((other, own), axis=1))

    sums = add(s05[:T], r1[0])
    sums_other = add(s05_other, r1[1])
    return (
        join(o_own, other[:, :HALF_Q]),
        join(dq_own, other[:, HALF_Q:2 * HALF_Q]),
        join(sums[:, :HALF_KV], sums_other[:, :HALF_KV]),
        join(sums[:, HALF_KV:], sums_other[:, HALF_KV:]),
    )


def solution(mesh):
    rows = P(("dp", "ctx"), None)
    return jax.shard_map(
        shards,
        mesh=mesh,
        in_specs=(rows, rows, rows, rows, P("dp"), P("dp")),
        out_specs=(rows, rows, rows, rows),
        check_vma=False,
    )
```

time: 161 us -> 105 us (0.65)
  the two profiles are of different devices: /device:TPU:27 before, /device:TPU:461 now
where the time goes in v2:
time: 105 us
  starting transfers between devices  59.1 us (56%)
  waiting for transfers between devices  28.5 us (27%)
  Pallas kernels  8.77 us (8%)
  other arithmetic  6.22 us (6%)
  local copies, waits for them, and re-layouts  1.27 us (1%)
    ppermute x12, starting transfers between devices, hop(): lax.ppermute(x, 'ctx', [(2 * a + c, 2 * b + (c ^ cross)) for a, b in pair...  49 us
    ppermute x12, waiting for transfers between devices, hop(): lax.ppermute(x, 'ctx', [(2 * a + c, 2 * b + (c ^ cross)) for a, b in pair...  26.8 us
    ppermute x3, starting transfers between devices, swap(): return lax.ppermute(x, 'ctx', [(i, i ^ 1) for i in range(2 * CHIPS)])  10.1 us
    pallas_call x6, Pallas kernels, call(): pl.pallas_call(body, grid_spec=pltpu.PrefetchScalarGridSpec(num_scalar_pr...  8.77 us
    select_n x4, other arithmetic, join(): jnp.where(core == 0, jnp.concatenate((own, other), axis=1), jnp.concatena...  3.22 us
    convert_element_type x6, other arithmetic, add(): return total.astype(jnp.bfloat16)  2.93 us
  transfers between devices with their start and end apart: 15, of which 7 were waited for; matrix products, arithmetic and copies ran while one was open for 4% of the time, Pallas kernels for 7%

profile of v2, /device:TPU:461, one launch (start us, length us, event | category | flops | bytes accessed | tf_op | source)
XLA Modules:
  0.0 104.8 jit_solution(1632192167890903557)
XLA Ops:
  0.7 1.1 %constant_dynamic-slice_fusion.4 = (bf16[128,1024]{1,0:T(8,128)(2,1)S(1)}, bf16[128,1024]{1,0:T(8,128)(2,1)S(1)}) fusion(bf16[128,2048]{1,0:T(8,128)(2,1)} %do_own.1, s32[]{:T(128)S(6)} %select_n.37, bf16[128,2048]{1,0:T(8,128)(2,1)} %q_own.1), kind=kLoop, calls=%fused_computation.16 | loop fusion | bytes 1048580 | tf_op jit(solution)/shard_map/dynamic_slice | solution.py:261
  1.8 0.0 copy-start
  1.8 0.0 copy-start.1
  1.9 0.0 copy-start.2
  1.9 0.0 copy-start.3
  1.9 2.7 %collective-permute-start = (bf16[128,2560]{1,0:T(8,128)(2,1)S(1)}, bf16[128,2560]{1,0:T(8,128)(2,1)S(1)}, u32[]{:S(2)}, u32[]{:S(2)}) collective-permute-start(bf16[128,2560]{1,0:T(8,128)(2,1)S(1)} %pad_maximum_fusion), channel_id=1, source_target_pairs={{0,1},{1,0},{2,3},{3,2},{4,5},{5,4},{6,7},{7,6},{8,9},{9,8},{10,11... | collective-permute-start | bytes 1966088 | tf_op jit(solution)/shard_map/ppermute | solution.py:248
  4.7 1.7 %collective-permute-done.other = bf16[128,2560]{1,0:T(8,128)(2,1)S(1)} collective-permute-done((bf16[128,2560]{1,0:T(8,128)(2,1)S(1)}, bf16[128,2560]{1,0:T(8,128)(2,1)S(1)}, u32[]{:S(2)}, u32[]{:S(2)}) %collective-permute-start) | collective-permute-done | bytes 655392 | tf_op jit(solution)/shard_map/ppermute | solution.py:248
  6.4 5.0 %collective-permute-start.3 = (bf16[256,512]{1,0:T(8,128)(2,1)S(1)}, bf16[256,512]{1,0:T(8,128)(2,1)S(1)}, u32[]{:S(2)}, u32[]{:S(2)}) collective-permute-start(bf16[256,512]{1,0:T(8,128)(2,1)S(1)} %pad_maximum_fusion.1.u_ref.refs_6_), channel_id=1, source_target_pairs={{0,12},{1,13},{2,14},{3,15},{4,0},{5,1},{6,2},{7,3},{16,28},{17,29... | collective-permute-start | bytes 786440 | tf_op jit(solution)/shard_map/ppermute | solution.py:240
  11.4 1.9 %collective-permute-start.1 = (bf16[256,512]{1,0:T(8,128)(2,1)S(1)}, bf16[256,512]{1,0:T(8,128)(2,1)S(1)}, u32[]{:S(2)}, u32[]{:S(2)}) collective-permute-start(bf16[256,512]{1,0:T(8,128)(2,1)S(1)} %pad_maximum_fusion.1.u_ref.refs_6_), channel_id=1, source_target_pairs={{0,2},{1,3},{2,4},{3,5},{4,6},{5,7},{6,8},{7,9},{8,10},{9,11},{10,... | collective-permute-start | bytes 786440 | tf_op jit(solution)/shard_map/ppermute | solution.py:240
  13.3 3.4 %collective-permute-done.3 = bf16[256,512]{1,0:T(8,128)(2,1)S(1)} collective-permute-done((bf16[256,512]{1,0:T(8,128)(2,1)S(1)}, bf16[256,512]{1,0:T(8,128)(2,1)S(1)}, u32[]{:S(2)}, u32[]{:S(2)}) %collective-permute-start.3) | collective-permute-done | bytes 262176 | tf_op jit(solution)/shard_map/ppermute | solution.py:240
  16.8 9.0 %collective-permute-start.4 = (bf16[256,512]{1,0:T(8,128)(2,1)S(1)}, bf16[256,512]{1,0:T(8,128)(2,1)S(1)}, u32[]{:S(2)}, u32[]{:S(2)}) collective-permute-start(bf16[256,512]{1,0:T(8,128)(2,1)S(1)} %collective-permute-done.3), channel_id=1, source_target_pairs={{12,10},{13,11},{14,12},{15,13},{0,14},{1,15},{2,0},{3,1},{28,26},... | collective-permute-start | bytes 786440 | tf_op jit(solution)/shard_map/ppermute | solution.py:240
  25.7 0.0 collective-permute-done.1.refs_0_.refs_5_
  25.8 1.3 %collective-permute-start.2 = (bf16[256,512]{1,0:T(8,128)(2,1)S(1)}, bf16[256,512]{1,0:T(8,128)(2,1)S(1)}, u32[]{:S(2)}, u32[]{:S(2)}) collective-permute-start(bf16[256,512]{1,0:T(8,128)(2,1)S(1)} %collective-permute-done.1.refs_0_.refs_5_), channel_id=1, source_target_pairs={{2,4},{3,5},{4,6},{5,7},{6,8},{7,9},{8,10},{9,11},{10,12},{11,13},... | collective-permute-start | bytes 786440 | tf_op jit(solution)/shard_map/ppermute | solution.py:240
  27.1 3.5 %collective-permute-done.4.refs_0_.refs_5_ = bf16[256,512]{1,0:T(8,128)(2,1)S(1)} collective-permute-done((bf16[256,512]{1,0:T(8,128)(2,1)S(1)}, bf16[256,512]{1,0:T(8,128)(2,1)S(1)}, u32[]{:S(2)}, u32[]{:S(2)}) %collective-permute-start.4) | collective-permute-done | bytes 262176 | tf_op jit(solution)/shard_map/ppermute | solution.py:240
  30.6 0.7 collective-permute-start.6
  31.2 0.7 collective-permute-done.2.refs_1_.refs_6_
  31.9 0.7 collective-permute-start.5
  32.6 2.2 %own.1 = (bf16[4,512,128]{2,1,0:T(8,128)(2,1)S(1)}, bf16[4,512,128]{2,1,0:T(8,128)(2,1)S(1)}, f32[4,8,512]{2,1,0:T(8,128)S(1)}, f32[4,8,512]{2,1,0:T(8,128)S(1)}, f32[4,128,512]{2,1,0:T(8,128)S(1)}) custom-call(s32[16]{0:T(128)S(1)} %copy-done.2, s32[16]{0:T(128)S(1)} %copy-done.3, s32[1]{0:T(128)} %bitcast.place, bf16[128,2048]{1,0:T(8,128)(2,1)S(1)} %copy-done, ...), custom_call_target="tpu_custom_call" | custom-call | flops 1024 | bytes 1024 | tf_op jit(solution)/shard_map/own/pallas_call | solution.py:221
  34.8 0.6 near.1
  35.5 0.6 far.1
  36.1 0.0 collective-permute-done.6.u4
  36.1 0.0 collective-permute-done.5.u3
  36.1 1.9 %middle.1 = (bf16[128,1024]{1,0:T(8,128)(2,1)S(1)}, bf16[128,1024]{1,0:T(8,128)(2,1)S(1)}, f32[4,8,512]{2,1,0:T(8,128)S(1)}, f32[4,8,512]{2,1,0:T(8,128)S(1)}, f...) custom-call(s32[16]{0:T(128)S(1)} %copy-done.2, s32[16]{0:T(128)S(1)} %copy-done.3, ...), custom_call_target="tpu_custom_call" | custom-call | flops 1024 | bytes 1024 | tf_op jit(solution)/shard_map/middle/pallas_call | solution.py:221
  38.0 0.7 collective-permute-start.8
  38.7 1.6 %collective-permute-start.7 = (bf16[256,512]{1,0:T(8,128)(2,1)}, bf16[256,512]{1,0:T(8,128)(2,1)}, u32[]{:S(2)}, u32[]{:S(2)}) collective-permute-start(bf16[256,512]{1,0:T(8,128)(2,1)} %get-tuple-element.47), channel_id=1, source_target_pairs={{8,10},{9,11},{10,12},{11,13},{12,14},{13,15},{14,0},{15,1},{24,26... | collective-permute-start | bytes 786440 | tf_op jit(solution)/shard_map/ppermute | solution.py:240
  40.2 0.7 back52.1
  40.9 0.0 collective-permute-done.8
  40.9 0.8 add_convert_fusion.2
  41.7 1.3 %collective-permute-start.11 = (bf16[256,512]{1,0:T(8,128)(2,1)}, bf16[256,512]{1,0:T(8,128)(2,1)}, u32[]{:S(2)}, u32[]{:S(2)}) collective-permute-start(bf16[256,512]{1,0:T(8,128)(2,1)} %add_convert_fusion.2), channel_id=1, source_target_pairs={{4,2},{5,3},{6,4},{7,5},{8,6},{9,7},{10,8},{11,9},{12,10},{13,11},... | collective-permute-start | bytes 786440 | tf_op jit(solution)/shard_map/ppermute | solution.py:240
  43.0 0.0 collective-permute-done.7
  43.0 1.0 add_convert_fusion.3
  44.0 1.3 %collective-permute-start.10 = (bf16[256,512]{1,0:T(8,128)(2,1)S(1)}, bf16[256,512]{1,0:T(8,128)(2,1)S(1)}, u32[]{:S(2)}, u32[]{:S(2)}) collective-permute-start(bf16[256,512]{1,0:T(8,128)(2,1)S(1)} %add_convert_fusion.3), channel_id=1, source_target_pairs={{10,0},{11,1},{12,2},{13,3},{14,4},{15,5},{0,6},{1,7},{26,16},{27,... | collective-permute-start | bytes 786440 | tf_op jit(solution)/shard_map/ppermute | solution.py:240
  45.3 2.7 %back10.1 = (bf16[256,512]{1,0:T(8,128)(2,1)S(1)}, bf16[256,512]{1,0:T(8,128)(2,1)S(1)}, bf16[128,1024]{1,0:T(8,128)(2,1)S(1)}, bf16[128,2048]{1,0:T(8,128)(2,1)S(1)}) custom-call(s32[16]{0:T(128)S(1)} %copy-done.2, s32[16]{0:T(128)S(1)} %copy-done.3, s32[1]{0:T(128)} %bitcast.place, bf16[4,512,128]{2,1,0:T(8,128)(2,1)S(1)} %get-tuple-element.30.q_ref.refs_0_, ...), custom_call_target="tpu_custom_call" | custom-call | flops 1024 | bytes 1024 | tf_op jit(solution)/shard_map/back10/pallas_call | solution.py:221
  48.1 3.6 %collective-permute-start.9 = (bf16[128,2048]{1,0:T(8,128)(2,1)S(1)}, bf16[128,2048]{1,0:T(8,128)(2,1)S(1)}, u32[]{:S(2)}, u32[]{:S(2)}) collective-permute-start(bf16[128,2048]{1,0:T(8,128)(2,1)S(1)} %get-tuple-element.52), channel_id=1, source_target_pairs={{0,1},{1,0},{2,3},{3,2},{4,5},{5,4},{6,7},{7,6},{8,9},{9,8},{10,11... | collective-permute-start | bytes 1572872 | tf_op jit(solution)/shard_map/ppermute | solution.py:248
  51.7 5.3 %collective-permute-done.11 = bf16[256,512]{1,0:T(8,128)(2,1)} collective-permute-done((bf16[256,512]{1,0:T(8,128)(2,1)}, bf16[256,512]{1,0:T(8,128)(2,1)}, u32[]{:S(2)}, u32[]{:S(2)}) %collective-permute-start.11) | collective-permute-done | bytes 262176 | tf_op jit(solution)/shard_map/ppermute | solution.py:240
  57.0 1.0 add_convert_fusion
  58.0 23.7 %collective-permute-start.12 = (bf16[128,512]{1,0:T(8,128)(2,1)S(1)}, bf16[128,512]{1,0:T(8,128)(2,1)S(1)}, u32[]{:S(2)}, u32[]{:S(2)}) collective-permute-start(bf16[128,512]{1,0:T(8,128)(2,1)S(1)} %get-tuple-element.58), channel_id=1, source_target_pairs={{2,0},{3,1},{4,2},{5,3},{6,4},{7,5},{8,6},{9,7},{10,8},{11,9},{12,... | collective-permute-start | bytes 393224 | tf_op jit(solution)/shard_map/ppermute | solution.py:240
  81.8 3.4 %collective-permute-done.10 = bf16[256,512]{1,0:T(8,128)(2,1)S(1)} collective-permute-done((bf16[256,512]{1,0:T(8,128)(2,1)S(1)}, bf16[256,512]{1,0:T(8,128)(2,1)S(1)}, u32[]{:S(2)}, u32[]{:S(2)}) %collective-permute-start.10) | collective-permute-done | bytes 262176 | tf_op jit(solution)/shard_map/ppermute | solution.py:240
  85.2 0.1 add_convert_fusion.1
  85.2 3.8 %collective-permute-start.13 = (bf16[128,512]{1,0:T(8,128)(2,1)S(1)}, bf16[128,512]{1,0:T(8,128)(2,1)S(1)}, u32[]{:S(2)}, u32[]{:S(2)}) collective-permute-start(bf16[128,512]{1,0:T(8,128)(2,1)S(1)} %slice.50), channel_id=1, source_target_pairs={{0,1},{1,0},{2,3},{3,2},{4,5},{5,4},{6,7},{7,6},{8,9},{9,8},{10,11... | collective-permute-start | bytes 393224 | tf_op jit(solution)/shard_map/ppermute | solution.py:248
  89.0 1.9 %collective-permute-start.14 = (bf16[128,512]{1,0:T(8,128)(2,1)S(1)}, bf16[128,512]{1,0:T(8,128)(2,1)S(1)}, u32[]{:S(2)}, u32[]{:S(2)}) collective-permute-start(bf16[128,512]{1,0:T(8,128)(2,1)S(1)} %get-tuple-element.59), channel_id=1, source_target_pairs={{2,1},{3,0},{4,3},{5,2},{6,5},{7,4},{8,7},{9,6},{10,9},{11,8},{12,... | collective-permute-start | bytes 393224 | tf_op jit(solution)/shard_map/ppermute | solution.py:240
  91.0 0.0 collective-permute-done.12
  91.0 10.5 %collective-permute-done.14 = bf16[128,512]{1,0:T(8,128)(2,1)S(1)} collective-permute-done((bf16[128,512]{1,0:T(8,128)(2,1)S(1)}, bf16[128,512]{1,0:T(8,128)(2,1)S(1)}, u32[]{:S(2)}, u32[]{:S(2)}) %collective-permute-start.14) | collective-permute-done | bytes 131104 | tf_op jit(solution)/shard_map/ppermute | solution.py:240
  101.6 0.7 maximum_select_fusion.3
  102.3 0.7 maximum_select_fusion.2
  103.0 0.0 collective-permute-done.9
  103.0 0.9 maximum_select_fusion.1
  103.9 0.9 maximum_select_fusion
  (20 shorter events, 0.3 us)
Async XLA Ops:
  0.6 1.1 %copy-start.4 = (bf16[128,512]{1,0:T(8,128)(2,1)S(1)}, bf16[128,512]{1,0:T(8,128)(2,1)}, u32[]{:S(2)}) copy-start(bf16[128,512]{1,0:T(8,128)(2,1)} %param.8) | copy-start | bytes 393220
  0.6 1.1 %copy-start.5 = (bf16[128,512]{1,0:T(8,128)(2,1)S(1)}, bf16[128,512]{1,0:T(8,128)(2,1)}, u32[]{:S(2)}) copy-start(bf16[128,512]{1,0:T(8,128)(2,1)} %param.7) | copy-start | bytes 393220
  1.8 30.7 %copy-start = (bf16[128,2048]{1,0:T(8,128)(2,1)S(1)}, bf16[128,2048]{1,0:T(8,128)(2,1)}, u32[]{:S(2)}) copy-start(bf16[128,2048]{1,0:T(8,128)(2,1)} %q_own.1) | copy-start | bytes 1572868
  1.8 30.7 %copy-start.1 = (bf16[128,2048]{1,0:T(8,128)(2,1)S(1)}, bf16[128,2048]{1,0:T(8,128)(2,1)}, u32[]{:S(2)}) copy-start(bf16[128,2048]{1,0:T(8,128)(2,1)} %do_own.1) | copy-start | bytes 1572868
  1.9 30.7 %copy-start.2 = (s32[16]{0:T(128)S(1)}, s32[16]{0:T(128)}, u32[]{:S(2)}) copy-start(s32[16]{0:T(128)} %docs.11) | copy-start | bytes 196
  1.9 30.7 %copy-start.3 = (s32[16]{0:T(128)S(1)}, s32[16]{0:T(128)}, u32[]{:S(2)}) copy-start(s32[16]{0:T(128)} %order.11) | copy-start | bytes 196
  1.9 4.4 %collective-permute-start = (bf16[128,2560]{1,0:T(8,128)(2,1)S(1)}, bf16[128,2560]{1,0:T(8,128)(2,1)S(1)}, u32[]{:S(2)}, u32[]{:S(2)}) collective-permute-start(bf16[128,2560]{1,0:T(8,128)(2,1)S(1)} %pad_maximum_fusion), channel_id=1, source_target_pairs={{0,1},{1,0},{2,3},{3,2},{4,5},{5,4},{6,7},{7,6},{8,9},{9,8},{10,11... | collective-permute-start | bytes 1966088 | tf_op jit(solution)/shard_map/ppermute | solution.py:248
  6.4 10.4 %collective-permute-start.3 = (bf16[256,512]{1,0:T(8,128)(2,1)S(1)}, bf16[256,512]{1,0:T(8,128)(2,1)S(1)}, u32[]{:S(2)}, u32[]{:S(2)}) collective-permute-start(bf16[256,512]{1,0:T(8,128)(2,1)S(1)} %pad_maximum_fusion.1.u_ref.refs_6_), channel_id=1, source_target_pairs={{0,12},{1,13},{2,14},{3,15},{4,0},{5,1},{6,2},{7,3},{16,28},{17,29... | collective-permute-start | bytes 786440 | tf_op jit(solution)/shard_map/ppermute | solution.py:240
  11.4 14.4 %collective-permute-start.1 = (bf16[256,512]{1,0:T(8,128)(2,1)S(1)}, bf16[256,512]{1,0:T(8,128)(2,1)S(1)}, u32[]{:S(2)}, u32[]{:S(2)}) collective-permute-start(bf16[256,512]{1,0:T(8,128)(2,1)S(1)} %pad_maximum_fusion.1.u_ref.refs_6_), channel_id=1, source_target_pairs={{0,2},{1,3},{2,4},{3,5},{4,6},{5,7},{6,8},{7,9},{8,10},{9,11},{10,... | collective-permute-start | bytes 786440 | tf_op jit(solution)/shard_map/ppermute | solution.py:240
  16.8 13.8 %collective-permute-start.4 = (bf16[256,512]{1,0:T(8,128)(2,1)S(1)}, bf16[256,512]{1,0:T(8,128)(2,1)S(1)}, u32[]{:S(2)}, u32[]{:S(2)}) collective-permute-start(bf16[256,512]{1,0:T(8,128)(2,1)S(1)} %collective-permute-done.3), channel_id=1, source_target_pairs={{12,10},{13,11},{14,12},{15,13},{0,14},{1,15},{2,0},{3,1},{28,26},... | collective-permute-start | bytes 786440 | tf_op jit(solution)/shard_map/ppermute | solution.py:240
  25.8 6.1 %collective-permute-start.2 = (bf16[256,512]{1,0:T(8,128)(2,1)S(1)}, bf16[256,512]{1,0:T(8,128)(2,1)S(1)}, u32[]{:S(2)}, u32[]{:S(2)}) collective-permute-start(bf16[256,512]{1,0:T(8,128)(2,1)S(1)} %collective-permute-done.1.refs_0_.refs_5_), channel_id=1, source_target_pairs={{2,4},{3,5},{4,6},{5,7},{6,8},{7,9},{8,10},{9,11},{10,12},{11,13},... | collective-permute-start | bytes 786440 | tf_op jit(solution)/shard_map/ppermute | solution.py:240
  30.6 5.6 %collective-permute-start.6 = (bf16[256,512]{1,0:T(8,128)(2,1)S(1)}, bf16[256,512]{1,0:T(8,128)(2,1)S(1)}, u32[]{:S(2)}, u32[]{:S(2)}) collective-permute-start(bf16[256,512]{1,0:T(8,128)(2,1)S(1)} %collective-permute-done.4.refs_0_.refs_5_), channel_id=1, source_target_pairs={{10,8},{11,9},{12,10},{13,11},{14,12},{15,13},{0,14},{1,15},{26,24... | collective-permute-start | bytes 786440 | tf_op jit(solution)/shard_map/ppermute | solution.py:240
  31.9 4.2 %collective-permute-start.5 = (bf16[256,512]{1,0:T(8,128)(2,1)S(1)}, bf16[256,512]{1,0:T(8,128)(2,1)S(1)}, u32[]{:S(2)}, u32[]{:S(2)}) collective-permute-start(bf16[256,512]{1,0:T(8,128)(2,1)S(1)} %collective-permute-done.2.refs_1_.refs_6_), channel_id=1, source_target_pairs={{4,6},{5,7},{6,8},{7,9},{8,10},{9,11},{10,12},{11,13},{12,14},{13,... | collective-permute-start | bytes 786440 | tf_op jit(solution)/shard_map/ppermute | solution.py:240
  38.0 2.9 %collective-permute-start.8 = (bf16[256,512]{1,0:T(8,128)(2,1)S(1)}, bf16[256,512]{1,0:T(8,128)(2,1)S(1)}, u32[]{:S(2)}, u32[]{:S(2)}) collective-permute-start(bf16[256,512]{1,0:T(8,128)(2,1)S(1)} %get-tuple-element.49), channel_id=1, source_target_pairs={{6,4},{7,5},{8,6},{9,7},{10,8},{11,9},{12,10},{13,11},{14,12},{15,... | collective-permute-start | bytes 786440 | tf_op jit(solution)/shard_map/ppermute | solution.py:240
  38.7 4.3 %collective-permute-start.7 = (bf16[256,512]{1,0:T(8,128)(2,1)}, bf16[256,512]{1,0:T(8,128)(2,1)}, u32[]{:S(2)}, u32[]{:S(2)}) collective-permute-start(bf16[256,512]{1,0:T(8,128)(2,1)} %get-tuple-element.47), channel_id=1, source_target_pairs={{8,10},{9,11},{10,12},{11,13},{12,14},{13,15},{14,0},{15,1},{24,26... | collective-permute-start | bytes 786440 | tf_op jit(solution)/shard_map/ppermute | solution.py:240
  41.7 15.3 %collective-permute-start.11 = (bf16[256,512]{1,0:T(8,128)(2,1)}, bf16[256,512]{1,0:T(8,128)(2,1)}, u32[]{:S(2)}, u32[]{:S(2)}) collective-permute-start(bf16[256,512]{1,0:T(8,128)(2,1)} %add_convert_fusion.2), channel_id=1, source_target_pairs={{4,2},{5,3},{6,4},{7,5},{8,6},{9,7},{10,8},{11,9},{12,10},{13,11},... | collective-permute-start | bytes 786440 | tf_op jit(solution)/shard_map/ppermute | solution.py:240
  44.0 41.1 %collective-permute-start.10 = (bf16[256,512]{1,0:T(8,128)(2,1)S(1)}, bf16[256,512]{1,0:T(8,128)(2,1)S(1)}, u32[]{:S(2)}, u32[]{:S(2)}) collective-permute-start(bf16[256,512]{1,0:T(8,128)(2,1)S(1)} %add_convert_fusion.3), channel_id=1, source_target_pairs={{10,0},{11,1},{12,2},{13,3},{14,4},{15,5},{0,6},{1,7},{26,16},{27,... | collective-permute-start | bytes 786440 | tf_op jit(solution)/shard_map/ppermute | solution.py:240
  48.1 54.9 %collective-permute-start.9 = (bf16[128,2048]{1,0:T(8,128)(2,1)S(1)}, bf16[128,2048]{1,0:T(8,128)(2,1)S(1)}, u32[]{:S(2)}, u32[]{:S(2)}) collective-permute-start(bf16[128,2048]{1,0:T(8,128)(2,1)S(1)} %get-tuple-element.52), channel_id=1, source_target_pairs={{0,1},{1,0},{2,3},{3,2},{4,5},{5,4},{6,7},{7,6},{8,9},{9,8},{10,11... | collective-permute-start | bytes 1572872 | tf_op jit(solution)/shard_map/ppermute | solution.py:248
  58.0 33.0 %collective-permute-start.12 = (bf16[128,512]{1,0:T(8,128)(2,1)S(1)}, bf16[128,512]{1,0:T(8,128)(2,1)S(1)}, u32[]{:S(2)}, u32[]{:S(2)}) collective-permute-start(bf16[128,512]{1,0:T(8,128)(2,1)S(1)} %get-tuple-element.58), channel_id=1, source_target_pairs={{2,0},{3,1},{4,2},{5,3},{6,4},{7,5},{8,6},{9,7},{10,8},{11,9},{12,... | collective-permute-start | bytes 393224 | tf_op jit(solution)/shard_map/ppermute | solution.py:240
  85.2 5.8 %collective-permute-start.13 = (bf16[128,512]{1,0:T(8,128)(2,1)S(1)}, bf16[128,512]{1,0:T(8,128)(2,1)S(1)}, u32[]{:S(2)}, u32[]{:S(2)}) collective-permute-start(bf16[128,512]{1,0:T(8,128)(2,1)S(1)} %slice.50), channel_id=1, source_target_pairs={{0,1},{1,0},{2,3},{3,2},{4,5},{5,4},{6,7},{7,6},{8,9},{9,8},{10,11... | collective-permute-start | bytes 393224 | tf_op jit(solution)/shard_map/ppermute | solution.py:248
  89.0 12.5 %collective-permute-start.14 = (bf16[128,512]{1,0:T(8,128)(2,1)S(1)}, bf16[128,512]{1,0:T(8,128)(2,1)S(1)}, u32[]{:S(2)}, u32[]{:S(2)}) collective-permute-start(bf16[128,512]{1,0:T(8,128)(2,1)S(1)} %get-tuple-element.59), channel_id=1, source_target_pairs={{2,1},{3,0},{4,3},{5,2},{6,5},{7,4},{8,7},{9,6},{10,9},{11,8},{12,... | collective-permute-start | bytes 393224 | tf_op jit(solution)/shard_map/ppermute | solution.py:240

commit v3 on v2

--- a/solution.py
+++ b/solution.py
@@ -163,7 +163,7 @@
     m_ref[...] = m_in[...]
     l_ref[...] = l_in[...]
     acc_ref[...] = acc_in[...]
-    forward_units((3, 4), (u3, u4), docs, order, me, q_ref, m_ref, l_ref, acc_ref)
+    forward_units((4,), (u4,), docs, order, me, q_ref, m_ref, l_ref, acc_ref)
     for chunk in range(CHUNKS):
         total = jnp.sum(l_ref[chunk], axis=0, keepdims=True)
         attn = (acc_ref[chunk] * (1.0 / total)).astype(jnp.bfloat16).astype(jnp.float32)
@@ -216,7 +216,11 @@
                     packed[:, HALF_Q + at:HALF_Q + at + D] = tile
 
 
-def call(body, name, scalars, operands, specs, outs, scratch=()):
+def sum_kernel(docs, order, place, a_ref, b_ref, out_ref):
+    out_ref[...] = (a_ref[...].astype(jnp.float32) + b_ref[...].astype(jnp.float32)).astype(jnp.bfloat16)
+
+
+def call(body, name, scalars, operands, specs, outs, scratch=(), flops=1024):
     whole = lambda shape: pl.BlockSpec(shape, lambda i, *_: (0,) * len(shape))
     return pl.pallas_call(
         body,
@@ -228,7 +232,7 @@
             scratch_shapes=list(scratch),
         ),
         out_shape=list(outs),
-        cost_estimate=pl.CostEstimate(flops=1024, bytes_accessed=1024, transcendentals=0),
+        cost_estimate=pl.CostEstimate(flops=flops, bytes_accessed=1024, transcendentals=0),
         compiler_params=pltpu.CompilerParams(
             dimension_semantics=("arbitrary",), vmem_limit_bytes=40 * 1024 * 1024
         ),
@@ -268,10 +272,7 @@
     u0 = jnp.concatenate((kv_own, across[:, 2 * HALF_Q:]), axis=0)
     u6 = hop(u0, [(s, (s + 6) % CHIPS) for s in range(4)])
     u1 = hop(u0, [(s, s + 1) for s in range(7)])
-    u5 = hop(u6, [((s + 6) % CHIPS, (s + 5) % CHIPS) for s in range(4)])
     u2 = hop(u1, [(s, s + 1) for s in range(1, 7)])
-    u3 = hop(u2, [(s, s + 1) for s in range(2, 7)])
-    u4 = hop(u5, [(s, (s - 1) % CHIPS) for s in (5, 6, 7, 0)])
 
     mine = pl.BlockSpec((T, HALF_Q), lambda i, d, o, p: (0, p[0] & 1))
     stats = struct((CHUNKS, 8, ROWS))
@@ -286,14 +287,19 @@
         first_kernel, "own", scalars, (query, output_gradient, across, u0),
         (mine, mine, None, None), (stacked, stacked, stats, stats, wide),
     )
-    m1, l1, acc1 = call(
-        functools.partial(near_kernel, (1, 2)), "near", scalars, (q, m0, l0, acc0, u1, u2), (None,) * 6,
-        (stats, stats, wide),
-    )
-    m2, l2, acc2 = call(
-        functools.partial(near_kernel, (5,)), "far", scalars, (q, m1, l1, acc1, u5), (None,) * 5,
-        (stats, stats, wide),
-    )
+    u5 = hop(after(u6, m0), [((s + 6) % CHIPS, (s + 5) % CHIPS) for s in range(4)])
+
+    def near(units, name, state, held_units, flops=1024):
+        return call(
+            functools.partial(near_kernel, units), name, scalars, (q, *state, *held_units),
+            (None,) * (4 + len(units)), (stats, stats, wide), flops=flops,
+        )
+
+    m1, l1, acc1 = near((1,), "near1", (m0, l0, acc0), (u1,))
+    u3 = hop(after(u2, m1), [(s, s + 1) for s in range(2, 7)])
+    u4 = hop(u5, [(s, (s - 1) % CHIPS) for s in (5, 6, 7, 0)])
+    state = near((2, 5), "near25", (m1, l1, acc1), (u2, u5))
+    m2, l2, acc2 = near((3,), "near3", state, (u3,), 1 << 31)
     o_own, o_send, lse, delta, dq3, g3, g4 = call(
         middle_kernel, "middle", scalars, (q, do, m2, l2, acc2, u3, u4), (None,) * 7,
         (token_half, token_half, stats, stats, wide, unit, unit), held,
@@ -317,24 +323,25 @@
     b3 = hop(g3, [(t, t - 1) for t in range(3, 8)])
     g5, g2, dq2 = back((5, 2), "back52", dq3, (u5, u2))
     a5 = add(g5, b4)
-    a2 = add(g2, b3)
+    a2 = add(g2, after(b3, a5))
     r5 = hop(a5, [(t, (t + 3) % CHIPS) for t in (5, 6, 7, 0)])
     b2 = hop(a2, [(t, t - 1) for t in range(2, 8)])
     g1, g0, dq_own, sent = back((1, 0), "back10", after(dq2, a5, a2), (u1, u0, o_send))
     a1 = add(g1, b2)
     r1 = [hop(a1[i * T:(i + 1) * T], [(t, t - 1) for t in range(1, 8)], i) for i in range(2)]
-    other = swap(sent)
-    s05 = add(g0, r5)
-    s05_other = swap(s05[T:])
-
+    s05, = call(sum_kernel, "sum05", scalars, (g0, r5), (None, None), (unit,), flops=3 << 31)
+    other = swap(after(sent, s05, r1[0], r1[1]))
     def join(own, other):
         return jnp.where(core == 0, jnp.concatenate((own, other), axis=1), jnp.concatenate((other, own), axis=1))
 
-    sums = add(s05[:T], r1[0])
+    attn = join(o_own, other[:, :HALF_Q])
+    grad_query = join(dq_own, other[:, HALF_Q:])
+    s05_other = swap(s05[T:])
+    sums = add(s05[:T], after(r1[0], r1[1]))
     sums_other = add(s05_other, r1[1])
     return (
-        join(o_own, other[:, :HALF_Q]),
-        join(dq_own, other[:, HALF_Q:2 * HALF_Q]),
+        attn,
+        grad_query,
         join(sums[:, :HALF_KV], sums_other[:, :HALF_KV]),
         join(sums[:, HALF_KV:], sums_other[:, HALF_KV:]),
     )

time: 105 us -> 94.1 us (0.90)
  the two profiles are of different devices: /device:TPU:461 before, /device:TPU:17 now
where the time goes in v3:
time: 94.1 us; the launch traced here: 93.5 us
  starting transfers between devices  39.2 us (42%)
  waiting for transfers between devices  30.8 us (33%)
  Pallas kernels  16 us (17%)
  other arithmetic  5.21 us (6%)
  local copies, waits for them, and re-layouts  1.27 us (1%)
  between operations  1.07 us (1%)
    ppermute x12, starting transfers between devices, hop(): lax.ppermute(x, 'ctx', [(2 * a + c, 2 * b + (c ^ cross)) for a, b in pair...  30.8 us
    ppermute x12, waiting for transfers between devices, hop(): lax.ppermute(x, 'ctx', [(2 * a + c, 2 * b + (c ^ cross)) for a, b in pair...  28.7 us
    pallas_call x8, Pallas kernels, call(): pl.pallas_call(body, grid_spec=pltpu.PrefetchScalarGridSpec(num_scalar_pr...  16 us
    ppermute x3, starting transfers between devices, swap(): return lax.ppermute(x, 'ctx', [(i, i ^ 1) for i in range(2 * CHIPS)])  8.37 us
    select_n x4, other arithmetic, join(): jnp.where(core == 0, jnp.concatenate((own, other), axis=1), jnp.concatena...  3.22 us
    ppermute x3, waiting for transfers between devices, swap(): return lax.ppermute(x, 'ctx', [(i, i ^ 1) for i in range(2 * CHIPS)])  2.07 us
    convert_element_type x5, other arithmetic, add(): return total.astype(jnp.bfloat16)  1.92 us
  transfers between devices with their start and end apart: 15, of which 8 were waited for; matrix products, arithmetic and copies ran while one was open for 3% of the time, Pallas kernels for 16%

profile of v3, /device:TPU:17, one launch (start us, length us, event | category | flops | bytes accessed | tf_op | source)
XLA Modules:
  0.0 93.5 jit_solution(15561616412412320689)
XLA Ops:
  0.7 1.1 %constant_dynamic-slice_fusion.4 = (bf16[128,1024]{1,0:T(8,128)(2,1)S(1)}, bf16[128,1024]{1,0:T(8,128)(2,1)S(1)}) fusion(bf16[128,2048]{1,0:T(8,128)(2,1)} %do_own.1, s32[]{:T(128)S(6)} %select_n.37, bf16[128,2048]{1,0:T(8,128)(2,1)} %q_own.1), kind=kLoop, calls=%fused_computation.15 | loop fusion | bytes 1048580 | tf_op jit(solution)/shard_map/dynamic_slice | solution.py:265
  1.8 0.0 copy-start
  1.8 0.0 copy-start.1
  1.9 0.0 copy-start.2
  1.9 0.0 copy-start.3
  1.9 2.7 %collective-permute-start = (bf16[128,2560]{1,0:T(8,128)(2,1)S(1)}, bf16[128,2560]{1,0:T(8,128)(2,1)S(1)}, u32[]{:S(2)}, u32[]{:S(2)}) collective-permute-start(bf16[128,2560]{1,0:T(8,128)(2,1)S(1)} %pad_maximum_fusion), channel_id=1, source_target_pairs={{0,1},{1,0},{2,3},{3,2},{4,5},{5,4},{6,7},{7,6},{8,9},{9,8},{10,11... | collective-permute-start | bytes 1966088 | tf_op jit(solution)/shard_map/ppermute | solution.py:252
  4.7 1.7 %collective-permute-done.other = bf16[128,2560]{1,0:T(8,128)(2,1)S(1)} collective-permute-done((bf16[128,2560]{1,0:T(8,128)(2,1)S(1)}, bf16[128,2560]{1,0:T(8,128)(2,1)S(1)}, u32[]{:S(2)}, u32[]{:S(2)}) %collective-permute-start) | collective-permute-done | bytes 655392 | tf_op jit(solution)/shard_map/ppermute | solution.py:252
  6.4 3.2 %collective-permute-start.1 = (bf16[256,512]{1,0:T(8,128)(2,1)S(1)}, bf16[256,512]{1,0:T(8,128)(2,1)S(1)}, u32[]{:S(2)}, u32[]{:S(2)}) collective-permute-start(bf16[256,512]{1,0:T(8,128)(2,1)S(1)} %pad_maximum_fusion.1.u_ref.refs_6_), channel_id=1, source_target_pairs={{0,2},{1,3},{2,4},{3,5},{4,6},{5,7},{6,8},{7,9},{8,10},{9,11},{10,... | collective-permute-start | bytes 786440 | tf_op jit(solution)/shard_map/ppermute | solution.py:244
  9.6 5.5 %collective-permute-start.3 = (bf16[256,512]{1,0:T(8,128)(2,1)S(1)}, bf16[256,512]{1,0:T(8,128)(2,1)S(1)}, u32[]{:S(2)}, u32[]{:S(2)}) collective-permute-start(bf16[256,512]{1,0:T(8,128)(2,1)S(1)} %pad_maximum_fusion.1.u_ref.refs_6_), channel_id=1, source_target_pairs={{0,12},{1,13},{2,14},{3,15},{4,0},{5,1},{6,2},{7,3},{16,28},{17,29... | collective-permute-start | bytes 786440 | tf_op jit(solution)/shard_map/ppermute | solution.py:244
  15.1 0.7 collective-permute-done.1.refs_0_.refs_5_
  15.8 3.5 %collective-permute-start.2 = (bf16[256,512]{1,0:T(8,128)(2,1)S(1)}, bf16[256,512]{1,0:T(8,128)(2,1)S(1)}, u32[]{:S(2)}, u32[]{:S(2)}) collective-permute-start(bf16[256,512]{1,0:T(8,128)(2,1)S(1)} %collective-permute-done.1.refs_0_.refs_5_), channel_id=1, source_target_pairs={{2,4},{3,5},{4,6},{5,7},{6,8},{7,9},{8,10},{9,11},{10,12},{11,13},... | collective-permute-start | bytes 786440 | tf_op jit(solution)/shard_map/ppermute | solution.py:244
  19.4 2.2 %own.1 = (bf16[4,512,128]{2,1,0:T(8,128)(2,1)S(1)}, bf16[4,512,128]{2,1,0:T(8,128)(2,1)S(1)}, f32[4,8,512]{2,1,0:T(8,128)S(1)}, f32[4,8,512]{2,1,0:T(8,128)S(1)}, f32[4,128,512]{2,1,0:T(8,128)S(1)}) custom-call(s32[16]{0:T(128)S(1)} %copy-done.2, s32[16]{0:T(128)S(1)} %copy-done.3, s32[1]{0:T(128)} %bitcast.place, bf16[128,2048]{1,0:T(8,128)(2,1)S(1)} %copy-done, ...), custom_call_target="tpu_custom_call" | custom-call | flops 1024 | bytes 1024 | tf_op jit(solution)/shard_map/own/pallas_call | solution.py:225
  21.6 3.2 %collective-permute-done.3 = bf16[256,512]{1,0:T(8,128)(2,1)S(1)} collective-permute-done((bf16[256,512]{1,0:T(8,128)(2,1)S(1)}, bf16[256,512]{1,0:T(8,128)(2,1)S(1)}, u32[]{:S(2)}, u32[]{:S(2)}) %collective-permute-start.3) | collective-permute-done | bytes 262176 | tf_op jit(solution)/shard_map/ppermute | solution.py:244
  24.8 0.7 collective-permute-start.4
  25.5 2.2 %near1.1 = (f32[4,8,512]{2,1,0:T(8,128)S(1)}, f32[4,8,512]{2,1,0:T(8,128)S(1)}, f32[4,128,512]{2,1,0:T(8,128)S(1)}) custom-call(s32[16]{0:T(128)S(1)} %copy-done.2, s32[16]{0:T(128)S(1)} %copy-done.3, s32[1]{0:T(128)} %bitcast.place, bf16[4,512,128]{2,1,0:T(8,128)(2,1)S(1)} %get-tuple-element.38.q_ref.refs_0_, f32[4,8,512]{2,1,0:T(8,128)S(1)} %get-tuple-element.40.m_in, ...), custom_call_target="tpu_custom_call" | custom-call | flops 1024 | bytes 1024 | tf_op jit(solution)/shard_map/near1/pallas_call | solution.py:225
  27.6 0.0 collective-permute-done.2.refs_0_.refs_6_
  27.6 2.2 %collective-permute-start.5 = (bf16[256,512]{1,0:T(8,128)(2,1)S(1)}, bf16[256,512]{1,0:T(8,128)(2,1)S(1)}, u32[]{:S(2)}, u32[]{:S(2)}) collective-permute-start(bf16[256,512]{1,0:T(8,128)(2,1)S(1)} %collective-permute-done.2.refs_0_.refs_6_), channel_id=1, source_target_pairs={{4,6},{5,7},{6,8},{7,9},{8,10},{9,11},{10,12},{11,13},{12,14},{13,... | collective-permute-start | bytes 786440 | tf_op jit(solution)/shard_map/ppermute | solution.py:244
  29.8 0.0 collective-permute-done.4.refs_1_.refs_5_
  29.8 0.7 collective-permute-start.6
  30.5 2.2 %near25.1 = (f32[4,8,512]{2,1,0:T(8,128)S(1)}, f32[4,8,512]{2,1,0:T(8,128)S(1)}, f32[4,128,512]{2,1,0:T(8,128)S(1)}) custom-call(s32[16]{0:T(128)S(1)} %copy-done.2, s32[16]{0:T(128)S(1)} %copy-done.3, s32[1]{0:T(128)} %bitcast.place, bf16[4,512,128]{2,1,0:T(8,128)(2,1)S(1)} %get-tuple-element.38.q_ref.refs_0_, f32[4,8,512]{2,1,0:T(8,128)S(1)} %get-tuple-element.43.m_in, ...), custom_call_target="tpu_custom_call" | custom-call | flops 1024 | bytes 1024 | tf_op jit(solution)/shard_map/near25/pallas_call | solution.py:225
  32.7 1.2 %collective-permute-done.5.refs_0_.u3 = bf16[256,512]{1,0:T(8,128)(2,1)S(1)} collective-permute-done((bf16[256,512]{1,0:T(8,128)(2,1)S(1)}, bf16[256,512]{1,0:T(8,128)(2,1)S(1)}, u32[]{:S(2)}, u32[]{:S(2)}) %collective-permute-start.5) | collective-permute-done | bytes 262176 | tf_op jit(solution)/shard_map/ppermute | solution.py:244
  33.9 0.6 near3.1
  34.5 0.0 collective-permute-done.6.u4
  34.5 1.2 %middle.1 = (bf16[128,1024]{1,0:T(8,128)(2,1)S(1)}, bf16[128,1024]{1,0:T(8,128)(2,1)S(1)}, f32[4,8,512]{2,1,0:T(8,128)S(1)}, f32[4,8,512]{2,1,0:T(8,128)S(1)}, f...) custom-call(s32[16]{0:T(128)S(1)} %copy-done.2, s32[16]{0:T(128)S(1)} %copy-done.3, ...), custom_call_target="tpu_custom_call" | custom-call | flops 1024 | bytes 1024 | tf_op jit(solution)/shard_map/middle/pallas_call | solution.py:225
  35.7 0.9 collective-permute-start.7
  36.6 1.3 %collective-permute-start.8 = (bf16[256,512]{1,0:T(8,128)(2,1)S(1)}, bf16[256,512]{1,0:T(8,128)(2,1)S(1)}, u32[]{:S(2)}, u32[]{:S(2)}) collective-permute-start(bf16[256,512]{1,0:T(8,128)(2,1)S(1)} %get-tuple-element.62), channel_id=1, source_target_pairs={{6,4},{7,5},{8,6},{9,7},{10,8},{11,9},{12,10},{13,11},{14,12},{15,... | collective-permute-start | bytes 786440 | tf_op jit(solution)/shard_map/ppermute | solution.py:244
  37.9 2.5 %back52.1 = (bf16[256,512]{1,0:T(8,128)(2,1)S(1)}, bf16[256,512]{1,0:T(8,128)(2,1)S(1)}, f32[4,128,512]{2,1,0:T(8,128)S(1)}) custom-call(s32[16]{0:T(128)S(1)} %copy-done.2, s32[16]{0:T(128)S(1)} %copy-done.3, s32[1]{0:T(128)} %bitcast.place, bf16[4,512,128]{2,1,0:T(8,128)(2,1)S(1)} %get-tuple-element.38.q_ref.refs_0_, ...), custom_call_target="tpu_custom_call" | custom-call | flops 1024 | bytes 1024 | tf_op jit(solution)/shard_map/back52/pallas_call | solution.py:225
  40.4 0.0 collective-permute-done.7
  40.4 0.1 add_convert_fusion.2
  40.4 7.3 %collective-permute-done.8 = bf16[256,512]{1,0:T(8,128)(2,1)S(1)} collective-permute-done((bf16[256,512]{1,0:T(8,128)(2,1)S(1)}, bf16[256,512]{1,0:T(8,128)(2,1)S(1)}, u32[]{:S(2)}, u32[]{:S(2)}) %collective-permute-start.8) | collective-permute-done | bytes 262176 | tf_op jit(solution)/shard_map/ppermute | solution.py:244
  47.8 0.8 add_convert_fusion.1
  48.5 1.9 %collective-permute-start.10 = (bf16[256,512]{1,0:T(8,128)(2,1)}, bf16[256,512]{1,0:T(8,128)(2,1)}, u32[]{:S(2)}, u32[]{:S(2)}) collective-permute-start(bf16[256,512]{1,0:T(8,128)(2,1)} %add_convert_fusion.1), channel_id=1, source_target_pairs={{4,2},{5,3},{6,4},{7,5},{8,6},{9,7},{10,8},{11,9},{12,10},{13,11},... | collective-permute-start | bytes 786440 | tf_op jit(solution)/shard_map/ppermute | solution.py:244
  50.5 1.3 %collective-permute-start.9 = (bf16[256,512]{1,0:T(8,128)(2,1)S(1)}, bf16[256,512]{1,0:T(8,128)(2,1)S(1)}, u32[]{:S(2)}, u32[]{:S(2)}) collective-permute-start(bf16[256,512]{1,0:T(8,128)(2,1)S(1)} %add_convert_fusion.2), channel_id=1, source_target_pairs={{10,0},{11,1},{12,2},{13,3},{14,4},{15,5},{0,6},{1,7},{26,16},{27,... | collective-permute-start | bytes 786440 | tf_op jit(solution)/shard_map/ppermute | solution.py:244
  51.8 4.6 %back10.1 = (bf16[256,512]{1,0:T(8,128)(2,1)S(1)}, bf16[256,512]{1,0:T(8,128)(2,1)S(1)}, bf16[128,1024]{1,0:T(8,128)(2,1)S(1)}, bf16[128,2048]{1,0:T(8,128)(2,1)S(1)}) custom-call(s32[16]{0:T(128)S(1)} %copy-done.2, s32[16]{0:T(128)S(1)} %copy-done.3, s32[1]{0:T(128)} %bitcast.place, bf16[4,512,128]{2,1,0:T(8,128)(2,1)S(1)} %get-tuple-element.38.q_ref.refs_0_, ...), custom_call_target="tpu_custom_call" | custom-call | flops 1024 | bytes 1024 | tf_op jit(solution)/shard_map/back10/pallas_call | solution.py:225
  56.3 12.4 %collective-permute-done.10 = bf16[256,512]{1,0:T(8,128)(2,1)} collective-permute-done((bf16[256,512]{1,0:T(8,128)(2,1)}, bf16[256,512]{1,0:T(8,128)(2,1)}, u32[]{:S(2)}, u32[]{:S(2)}) %collective-permute-start.10) | collective-permute-done | bytes 262176 | tf_op jit(solution)/shard_map/ppermute | solution.py:244
  68.7 1.0 %add_convert_fusion = bf16[256,512]{1,0:T(8,128)(2,1)S(1)} fusion(bf16[256,512]{1,0:T(8,128)(2,1)} %collective-permute-done.10, bf16[256,512]{1,0:T(8,128)(2,1)S(1)} %get-tuple-element.68), kind=kLoop, calls=%fused_computation.3 | loop fusion | flops 524288 | bytes 786432 | tf_op jit(solution)/shard_map/convert_element_type | solution.py:320
  69.8 1.9 %collective-permute-start.12 = (bf16[128,512]{1,0:T(8,128)(2,1)S(1)}, bf16[128,512]{1,0:T(8,128)(2,1)S(1)}, u32[]{:S(2)}, u32[]{:S(2)}) collective-permute-start(bf16[128,512]{1,0:T(8,128)(2,1)S(1)} %get-tuple-element.74), channel_id=1, source_target_pairs={{2,1},{3,0},{4,3},{5,2},{6,5},{7,4},{8,7},{9,6},{10,9},{11,8},{12,... | collective-permute-start | bytes 393224 | tf_op jit(solution)/shard_map/ppermute | solution.py:244
  71.7 7.9 %collective-permute-start.11 = (bf16[128,512]{1,0:T(8,128)(2,1)S(1)}, bf16[128,512]{1,0:T(8,128)(2,1)S(1)}, u32[]{:S(2)}, u32[]{:S(2)}) collective-permute-start(bf16[128,512]{1,0:T(8,128)(2,1)S(1)} %get-tuple-element.75), channel_id=1, source_target_pairs={{2,0},{3,1},{4,2},{5,3},{6,4},{7,5},{8,6},{9,7},{10,8},{11,9},{12,... | collective-permute-start | bytes 393224 | tf_op jit(solution)/shard_map/ppermute | solution.py:244
  79.6 3.9 %collective-permute-done.9.b_ref = bf16[256,512]{1,0:T(8,128)(2,1)S(1)} collective-permute-done((bf16[256,512]{1,0:T(8,128)(2,1)S(1)}, bf16[256,512]{1,0:T(8,128)(2,1)S(1)}, u32[]{:S(2)}, u32[]{:S(2)}) %collective-permute-start.9) | collective-permute-done | bytes 262176 | tf_op jit(solution)/shard_map/ppermute | solution.py:244
  83.4 0.6 sum05.1
  84.1 3.7 %collective-permute-start.14 = (bf16[128,512]{1,0:T(8,128)(2,1)S(1)}, bf16[128,512]{1,0:T(8,128)(2,1)S(1)}, u32[]{:S(2)}, u32[]{:S(2)}) collective-permute-start(bf16[128,512]{1,0:T(8,128)(2,1)S(1)} %slice.51), channel_id=1, source_target_pairs={{0,1},{1,0},{2,3},{3,2},{4,5},{5,4},{6,7},{7,6},{8,9},{9,8},{10,11... | collective-permute-start | bytes 393224 | tf_op jit(solution)/shard_map/ppermute | solution.py:252
  87.8 0.0 collective-permute-done.12
  87.8 1.9 %collective-permute-start.13 = (bf16[128,2048]{1,0:T(8,128)(2,1)S(1)}, bf16[128,2048]{1,0:T(8,128)(2,1)S(1)}, u32[]{:S(2)}, u32[]{:S(2)}) collective-permute-start(bf16[128,2048]{1,0:T(8,128)(2,1)S(1)} %get-tuple-element.69), channel_id=1, source_target_pairs={{0,1},{1,0},{2,3},{3,2},{4,5},{5,4},{6,7},{7,6},{8,9},{9,8},{10,11... | collective-permute-start | bytes 1572872 | tf_op jit(solution)/shard_map/ppermute | solution.py:252
  89.9 0.7 maximum_select_fusion.3
  90.6 0.7 maximum_select_fusion.2
  91.3 0.4 collective-permute-done.13
  91.7 0.9 maximum_select_fusion.1
  92.6 0.9 maximum_select_fusion
  (21 shorter events, 0.3 us)
Async XLA Ops:
  0.6 1.1 %copy-start.4 = (bf16[128,512]{1,0:T(8,128)(2,1)S(1)}, bf16[128,512]{1,0:T(8,128)(2,1)}, u32[]{:S(2)}) copy-start(bf16[128,512]{1,0:T(8,128)(2,1)} %param.8) | copy-start | bytes 393220
  0.6 1.1 %copy-start.5 = (bf16[128,512]{1,0:T(8,128)(2,1)S(1)}, bf16[128,512]{1,0:T(8,128)(2,1)}, u32[]{:S(2)}) copy-start(bf16[128,512]{1,0:T(8,128)(2,1)} %param.7) | copy-start | bytes 393220
  1.8 17.5 %copy-start = (bf16[128,2048]{1,0:T(8,128)(2,1)S(1)}, bf16[128,2048]{1,0:T(8,128)(2,1)}, u32[]{:S(2)}) copy-start(bf16[128,2048]{1,0:T(8,128)(2,1)} %q_own.1) | copy-start | bytes 1572868
  1.8 17.5 %copy-start.1 = (bf16[128,2048]{1,0:T(8,128)(2,1)S(1)}, bf16[128,2048]{1,0:T(8,128)(2,1)}, u32[]{:S(2)}) copy-start(bf16[128,2048]{1,0:T(8,128)(2,1)} %do_own.1) | copy-start | bytes 1572868
  1.9 17.5 %copy-start.2 = (s32[16]{0:T(128)S(1)}, s32[16]{0:T(128)}, u32[]{:S(2)}) copy-start(s32[16]{0:T(128)} %docs.15) | copy-start | bytes 196
  1.9 17.5 %copy-start.3 = (s32[16]{0:T(128)S(1)}, s32[16]{0:T(128)}, u32[]{:S(2)}) copy-start(s32[16]{0:T(128)} %order.15) | copy-start | bytes 196
  1.9 4.4 %collective-permute-start = (bf16[128,2560]{1,0:T(8,128)(2,1)S(1)}, bf16[128,2560]{1,0:T(8,128)(2,1)S(1)}, u32[]{:S(2)}, u32[]{:S(2)}) collective-permute-start(bf16[128,2560]{1,0:T(8,128)(2,1)S(1)} %pad_maximum_fusion), channel_id=1, source_target_pairs={{0,1},{1,0},{2,3},{3,2},{4,5},{5,4},{6,7},{7,6},{8,9},{9,8},{10,11... | collective-permute-start | bytes 1966088 | tf_op jit(solution)/shard_map/ppermute | solution.py:252
  6.4 9.4 %collective-permute-start.1 = (bf16[256,512]{1,0:T(8,128)(2,1)S(1)}, bf16[256,512]{1,0:T(8,128)(2,1)S(1)}, u32[]{:S(2)}, u32[]{:S(2)}) collective-permute-start(bf16[256,512]{1,0:T(8,128)(2,1)S(1)} %pad_maximum_fusion.1.u_ref.refs_6_), channel_id=1, source_target_pairs={{0,2},{1,3},{2,4},{3,5},{4,6},{5,7},{6,8},{7,9},{8,10},{9,11},{10,... | collective-permute-start | bytes 786440 | tf_op jit(solution)/shard_map/ppermute | solution.py:244
  9.6 15.2 %collective-permute-start.3 = (bf16[256,512]{1,0:T(8,128)(2,1)S(1)}, bf16[256,512]{1,0:T(8,128)(2,1)S(1)}, u32[]{:S(2)}, u32[]{:S(2)}) collective-permute-start(bf16[256,512]{1,0:T(8,128)(2,1)S(1)} %pad_maximum_fusion.1.u_ref.refs_6_), channel_id=1, source_target_pairs={{0,12},{1,13},{2,14},{3,15},{4,0},{5,1},{6,2},{7,3},{16,28},{17,29... | collective-permute-start | bytes 786440 | tf_op jit(solution)/shard_map/ppermute | solution.py:244
  15.8 11.8 %collective-permute-start.2 = (bf16[256,512]{1,0:T(8,128)(2,1)S(1)}, bf16[256,512]{1,0:T(8,128)(2,1)S(1)}, u32[]{:S(2)}, u32[]{:S(2)}) collective-permute-start(bf16[256,512]{1,0:T(8,128)(2,1)S(1)} %collective-permute-done.1.refs_0_.refs_5_), channel_id=1, source_target_pairs={{2,4},{3,5},{4,6},{5,7},{6,8},{7,9},{8,10},{9,11},{10,12},{11,13},... | collective-permute-start | bytes 786440 | tf_op jit(solution)/shard_map/ppermute | solution.py:244
  24.8 5.0 %collective-permute-start.4 = (bf16[256,512]{1,0:T(8,128)(2,1)S(1)}, bf16[256,512]{1,0:T(8,128)(2,1)S(1)}, u32[]{:S(2)}, u32[]{:S(2)}) collective-permute-start(bf16[256,512]{1,0:T(8,128)(2,1)S(1)} %collective-permute-done.3), channel_id=1, source_target_pairs={{12,10},{13,11},{14,12},{15,13},{0,14},{1,15},{2,0},{3,1},{28,26},... | collective-permute-start | bytes 786440 | tf_op jit(solution)/shard_map/ppermute | solution.py:244
  27.6 6.3 %collective-permute-start.5 = (bf16[256,512]{1,0:T(8,128)(2,1)S(1)}, bf16[256,512]{1,0:T(8,128)(2,1)S(1)}, u32[]{:S(2)}, u32[]{:S(2)}) collective-permute-start(bf16[256,512]{1,0:T(8,128)(2,1)S(1)} %collective-permute-done.2.refs_0_.refs_6_), channel_id=1, source_target_pairs={{4,6},{5,7},{6,8},{7,9},{8,10},{9,11},{10,12},{11,13},{12,14},{13,... | collective-permute-start | bytes 786440 | tf_op jit(solution)/shard_map/ppermute | solution.py:244
  29.8 4.7 %collective-permute-start.6 = (bf16[256,512]{1,0:T(8,128)(2,1)S(1)}, bf16[256,512]{1,0:T(8,128)(2,1)S(1)}, u32[]{:S(2)}, u32[]{:S(2)}) collective-permute-start(bf16[256,512]{1,0:T(8,128)(2,1)S(1)} %collective-permute-done.4.refs_1_.refs_5_), channel_id=1, source_target_pairs={{10,8},{11,9},{12,10},{13,11},{14,12},{15,13},{0,14},{1,15},{26,24... | collective-permute-start | bytes 786440 | tf_op jit(solution)/shard_map/ppermute | solution.py:244
  35.7 4.7 %collective-permute-start.7 = (bf16[256,512]{1,0:T(8,128)(2,1)S(1)}, bf16[256,512]{1,0:T(8,128)(2,1)S(1)}, u32[]{:S(2)}, u32[]{:S(2)}) collective-permute-start(bf16[256,512]{1,0:T(8,128)(2,1)S(1)} %get-tuple-element.60), channel_id=1, source_target_pairs={{8,10},{9,11},{10,12},{11,13},{12,14},{13,15},{14,0},{15,1},{24,26... | collective-permute-start | bytes 786440 | tf_op jit(solution)/shard_map/ppermute | solution.py:244
  36.6 11.2 %collective-permute-start.8 = (bf16[256,512]{1,0:T(8,128)(2,1)S(1)}, bf16[256,512]{1,0:T(8,128)(2,1)S(1)}, u32[]{:S(2)}, u32[]{:S(2)}) collective-permute-start(bf16[256,512]{1,0:T(8,128)(2,1)S(1)} %get-tuple-element.62), channel_id=1, source_target_pairs={{6,4},{7,5},{8,6},{9,7},{10,8},{11,9},{12,10},{13,11},{14,12},{15,... | collective-permute-start | bytes 786440 | tf_op jit(solution)/shard_map/ppermute | solution.py:244
  48.5 20.2 %collective-permute-start.10 = (bf16[256,512]{1,0:T(8,128)(2,1)}, bf16[256,512]{1,0:T(8,128)(2,1)}, u32[]{:S(2)}, u32[]{:S(2)}) collective-permute-start(bf16[256,512]{1,0:T(8,128)(2,1)} %add_convert_fusion.1), channel_id=1, source_target_pairs={{4,2},{5,3},{6,4},{7,5},{8,6},{9,7},{10,8},{11,9},{12,10},{13,11},... | collective-permute-start | bytes 786440 | tf_op jit(solution)/shard_map/ppermute | solution.py:244
  50.5 33.0 %collective-permute-start.9 = (bf16[256,512]{1,0:T(8,128)(2,1)S(1)}, bf16[256,512]{1,0:T(8,128)(2,1)S(1)}, u32[]{:S(2)}, u32[]{:S(2)}) collective-permute-start(bf16[256,512]{1,0:T(8,128)(2,1)S(1)} %add_convert_fusion.2), channel_id=1, source_target_pairs={{10,0},{11,1},{12,2},{13,3},{14,4},{15,5},{0,6},{1,7},{26,16},{27,... | collective-permute-start | bytes 786440 | tf_op jit(solution)/shard_map/ppermute | solution.py:244
  69.8 18.0 %collective-permute-start.12 = (bf16[128,512]{1,0:T(8,128)(2,1)S(1)}, bf16[128,512]{1,0:T(8,128)(2,1)S(1)}, u32[]{:S(2)}, u32[]{:S(2)}) collective-permute-start(bf16[128,512]{1,0:T(8,128)(2,1)S(1)} %get-tuple-element.74), channel_id=1, source_target_pairs={{2,1},{3,0},{4,3},{5,2},{6,5},{7,4},{8,7},{9,6},{10,9},{11,8},{12,... | collective-permute-start | bytes 393224 | tf_op jit(solution)/shard_map/ppermute | solution.py:244
  71.7 16.1 %collective-permute-start.11 = (bf16[128,512]{1,0:T(8,128)(2,1)S(1)}, bf16[128,512]{1,0:T(8,128)(2,1)S(1)}, u32[]{:S(2)}, u32[]{:S(2)}) collective-permute-start(bf16[128,512]{1,0:T(8,128)(2,1)S(1)} %get-tuple-element.75), channel_id=1, source_target_pairs={{2,0},{3,1},{4,2},{5,3},{6,4},{7,5},{8,6},{9,7},{10,8},{11,9},{12,... | collective-permute-start | bytes 393224 | tf_op jit(solution)/shard_map/ppermute | solution.py:244
  84.1 5.7 %collective-permute-start.14 = (bf16[128,512]{1,0:T(8,128)(2,1)S(1)}, bf16[128,512]{1,0:T(8,128)(2,1)S(1)}, u32[]{:S(2)}, u32[]{:S(2)}) collective-permute-start(bf16[128,512]{1,0:T(8,128)(2,1)S(1)} %slice.51), channel_id=1, source_target_pairs={{0,1},{1,0},{2,3},{3,2},{4,5},{5,4},{6,7},{7,6},{8,9},{9,8},{10,11... | collective-permute-start | bytes 393224 | tf_op jit(solution)/shard_map/ppermute | solution.py:252
  87.8 3.8 %collective-permute-start.13 = (bf16[128,2048]{1,0:T(8,128)(2,1)S(1)}, bf16[128,2048]{1,0:T(8,128)(2,1)S(1)}, u32[]{:S(2)}, u32[]{:S(2)}) collective-permute-start(bf16[128,2048]{1,0:T(8,128)(2,1)S(1)} %get-tuple-element.69), channel_id=1, source_target_pairs={{0,1},{1,0},{2,3},{3,2},{4,5},{5,4},{6,7},{7,6},{8,9},{9,8},{10,11... | collective-permute-start | bytes 1572872 | tf_op jit(solution)/shard_map/ppermute | solution.py:252
